TPU v7x, 256 devices: a whole 4x4x8 slice. The times are simulated.
256 devices in a mesh: group: 8 (over y_lo, x), leaf: 32 (over z, y_hi, core).
Axes of the slice: x: 4, y: 4 (y_hi: 2, y_lo: 2; y = y_hi * 2 + y_lo), z: 8, core: 2. Of those that a mesh axis runs over, the one named last changes fastest.
Arguments:
- points: bfloat16 [262144, 128], P(('group', 'leaf')), may hold values from -7 to 7
- vectors: bfloat16 [262144, 64], P(('group', 'leaf')), may hold values from -1.5 to 1.5
- leaf_interp: bfloat16 [262144, 128], P(('group', 'leaf')), may hold values from -0.5 to 0.5
- leaf_skeleton: int32 [32768], P(('group', 'leaf')), may hold values from 0 to 1023, as said below
- group_transfer: bfloat16 [32768, 512], P(('group', 'leaf')), may hold values from -0.25 to 0.25
- group_skeleton: int32 [4096], P('group'), may hold values from 0 to 4095, as said below
Outputs:
- product: float32 [262144, 64], P(('group', 'leaf'))
- basis: float32 [262144, 64], P(('group', 'leaf'))
Inputs may be any that keep to these rules, and one draw needn't show every extreme that they name: `leaf_skeleton`: each leaf's 128 entries are different positions among that leaf's 1024 points, in ascending order. `group_skeleton`: each group's 512 entries are different positions, in ascending order, among the group's leaf skeleton points, numbered leaf by leaf with 128 to a leaf.
All inputs are finite; a program needn't handle non-finite values.
Results may differ from a plain program's by a relative error of at most 0.0081.
Values may be sent and summed in bfloat16 or wider, within the bound.
A program may use at most 64 MiB of HBM per device.

v0:
```python
import math

import jax
import jax.numpy as jnp
from jax import lax
from jax.sharding import PartitionSpec as P


def swapped(value, axis, distance):
    mask = 2**distance
    pairs = [(source, source ^ mask) for source in range(lax.axis_size(axis))]
    return lax.ppermute(value, axis, pairs)


def apply_kernel(queries, query_norms, key_rows, weights):
    width = queries.shape[1]
    row_count = queries.shape[0]
    block_rows = math.gcd(row_count, 512)
    key_norm_values = jnp.sum(jnp.square(key_rows.astype(jnp.float32)), axis=1)
    query_blocks = queries.reshape(row_count // block_rows, block_rows, width)
    norm_blocks = query_norms.reshape(row_count // block_rows, block_rows)

    def one_block(block_pair):
        block_queries, block_norms = block_pair
        inner_prod = lax.dot_general(
            block_queries, key_rows, (((1,), (1,)), ((), ())), preferred_element_type=jnp.float32
        )
        squared_distance = block_norms[:, None] + key_norm_values[None, :] - 2.0 * inner_prod
        kernel_vals = jnp.exp(squared_distance * (-2.0 / width)).astype(jnp.bfloat16)
        return jnp.dot(kernel_vals, weights, preferred_element_type=jnp.float32)

    return lax.map(one_block, (query_blocks, norm_blocks)).reshape(row_count, weights.shape[1])


def per_device(points, vectors, leaf_interp, leaf_skeleton, group_transfer, group_skeleton):
    row_count = points.shape[0]
    width = points.shape[1]
    skel_count = leaf_skeleton.shape[0]
    group_total = group_skeleton.shape[0]
    leaf_number = lax.axis_index("leaf")
    group_index = lax.axis_index("group")
    point_norms = jnp.sum(jnp.square(points.astype(jnp.float32)), axis=1)
    skel_points = jnp.take(points, leaf_skeleton, axis=0)
    skeleton_weight = lax.dot_general(
        leaf_interp, vectors, (((0,), (0,)), ((), ())), preferred_element_type=jnp.float32
    ).astype(jnp.bfloat16)
    partner = swapped(jnp.concatenate([points, vectors], axis=1), "leaf", 0)
    running = apply_kernel(points, point_norms, points, vectors)
    running = running + apply_kernel(points, point_norms, partner[:, :width], partner[:, width:])
    gathered_points, gathered_weights = (
        lax.all_gather(skel_points, "leaf", axis=0, tiled=True),
        lax.all_gather(skeleton_weight, "leaf", axis=0, tiled=True),
    )
    owning_leaf = lax.iota(jnp.int32, gathered_points.shape[0]) // skel_count
    kept_leaves = (owning_leaf != leaf_number) & (owning_leaf != leaf_number ^ 1)
    near_weights = jnp.where(
        kept_leaves[:, None], gathered_weights, jnp.zeros_like(gathered_weights)
    )
    running = running + apply_kernel(points, point_norms, gathered_points, near_weights)
    weight_term = lax.dot_general(
        group_transfer,
        skeleton_weight,
        (((0,), (0,)), ((), ())),
        preferred_element_type=jnp.float32,
    )
    group_points = jnp.take(gathered_points, group_skeleton, axis=0)
    weight_whole = lax.psum(weight_term, "leaf")
    key_rows = lax.all_gather(group_points, "group", axis=0, tiled=True)
    weights = lax.all_gather(weight_whole.astype(jnp.bfloat16), "group", axis=0, tiled=True)
    owner_group = lax.iota(jnp.int32, key_rows.shape[0]) // group_total
    kept_rows = owner_group != group_index
    weights = jnp.where(kept_rows[:, None], weights, jnp.zeros_like(weights))
    running = running + apply_kernel(points, point_norms, key_rows, weights)
    gram_local = lax.dot_general(
        running, running, (((0,), (0,)), ((), ())), precision=lax.Precision.HIGHEST
    )
    gram_whole = lax.psum(gram_local, ("group", "leaf"))
    lower = jnp.linalg.cholesky(gram_whole)
    solved = jax.scipy.linalg.solve_triangular(lower, running.T, lower=True).T
    scale = math.sqrt(row_count * lax.axis_size("group") * lax.axis_size("leaf"))
    return (running, solved * scale)


def solution(mesh):
    return jax.shard_map(
        per_device,
        mesh=mesh,
        in_specs=(
            P(("group", "leaf"), None),
            P(("group", "leaf"), None),
            P(("group", "leaf"), None),
            P(("group", "leaf")),
            P(("group", "leaf"), None),
            P("group"),
        ),
        out_specs=(P(("group", "leaf"), None), P(("group", "leaf"), None)),
        check_vma=False,
    )
```

profile of v0, /device:TPU:1, one launch (start us, length us, event | category | flops | bytes accessed | tf_op | source)
XLA Modules:
  0.0 372.5 jit_solution(5917678524635661892)
XLA Ops:
  8.6 1.7 gather_fusion
  12.2 1.1 pad_maximum_fusion
  13.3 3.3 collective-permute-start
  17.0 44.5 %all_gather.13 = bf16[4096,64]{0,1:T(8,128)(2,1)S(1)} all-gather(bf16[128,64]{0,1:T(8,128)(2,1)S(1)} %convolution_convert_fusion), channel_id=1, replica_groups=mesh['group'=8,'leaf'=32] {'leaf'}, dimensions={0}, use_global_device_ids=true | all-gather | bytes 540672 | tf_op jit(solution)/shard_map/all_gather | solution.py:52
  61.7 1.8 while.40
  63.5 123.2 %all-reduce.1 = bf16[512,64]{0,1:T(8,128)(2,1)S(1)} all-reduce(f32[512,64]{0,1:T(8,128)S(1)} %convolution_bitcast_fusion), channel_id=1, replica_groups=mesh['group'=8,'leaf'=32] {'leaf'}, use_global_device_ids=true, to_apply=%region_10.11 | all-reduce | flops 32768 | bytes 196608 | tf_op jit(solution)/shard_map/psum | solution.py:67
  186.7 23.1 %all_gather.15 = bf16[4096,64]{0,1:T(8,128)(2,1)S(1)} all-gather(bf16[512,64]{0,1:T(8,128)(2,1)S(1)} %all-reduce.1), channel_id=1, replica_groups=mesh['group'=8,'leaf'=32] {'group'}, dimensions={0}, use_global_device_ids=true | all-gather | bytes 589824 | tf_op jit(solution)/shard_map/all_gather | solution.py:69
  209.9 1.4 copy.9
  213.5 2.4 gather_fusion.1
  216.8 3.8 %while.41 = (s32[]{:T(128)}, f32[2,512,64]{1,2,0:T(8,128)S(1)}, f32[2,512]{1,0:T(2,128)S(1)}, f32[1024]{0:T(1024)S(1)}, bf16[2,512,128]{2,1,0:T(8,128)(2,1)S(1)}...) while((s32[]{:T(128)}, f32[2,512,64]{1,2,0:T(8,128)S(1)}, ...), condition=%wide.region_5.6_spmd, body=%wide.region_4.5_spmd.sunk | while | flops 203948032 | bytes 797785 | solution.py:32
  216.8 1.9 fusion.102
  218.8 1.8 fusion.102
  221.2 8.6 %while.42 = (s32[]{:T(128)}, f32[2,512,64]{1,2,0:T(8,128)S(1)}, f32[2,512]{1,0:T(2,128)S(1)}, f32[4096]{0:T(1024)S(1)}, bf16[2,512,128]{2,1,0:T(8,128)(2,1)S(1)}...) while((s32[]{:T(128)}, f32[2,512,64]{1,2,0:T(8,128)S(1)}, ...), condition=%wide.region_8.9_spmd, body=%wide.region_7.8_spmd.sunk | while | flops 815792128 | bytes 2382937 | solution.py:32
  221.3 4.3 %fusion.106 = f32[2,512,64]{1,2,0:T(8,128)S(1)} fusion(f32[2,512,64]{1,2,0:T(8,128)S(1)} %get-tuple-element.429, s32[]{:T(128)} %get-tuple-element.428, bf16[4096,64]{1,0:T(8,128)(2,1)} %get-tuple-element.442, bf16[4096,128]{1,0:T(8,128)(2,1)S(1)} %get-tuple-element.441, f32[4096]{0:T(1024)S(1)} %get-tuple-element.439, f32[512]{0:T(512)S(1)} %bitcast.116, ...), kind=kOutput, calls=%fused_computation.33.clone.1 | convolution fusion | flops 815792128 | bytes 2378752 | tf_op jit(solution)/shard_map/while/body/eval_jaxpr/dot_general | solution.py:30
  225.6 4.3 %fusion.106 = f32[2,512,64]{1,2,0:T(8,128)S(1)} fusion(f32[2,512,64]{1,2,0:T(8,128)S(1)} %get-tuple-element.429, s32[]{:T(128)} %get-tuple-element.428, bf16[4096,64]{1,0:T(8,128)(2,1)} %get-tuple-element.442, bf16[4096,128]{1,0:T(8,128)(2,1)S(1)} %get-tuple-element.441, f32[4096]{0:T(1024)S(1)} %get-tuple-element.439, f32[512]{0:T(512)S(1)} %bitcast.116, ...), kind=kOutput, calls=%fused_computation.33.clone.1 | convolution fusion | flops 815792128 | bytes 2378752 | tf_op jit(solution)/shard_map/while/body/eval_jaxpr/dot_general | solution.py:30
  229.9 30.6 %all-gather.5.cloned.1.call-done = bf16[4096,128]{1,0:T(8,128)(2,1)} async-done(((bf16[512,128]{1,0:T(8,128)(2,1)}), bf16[4096,128]{1,0:T(8,128)(2,1)}) %all-gather.5.cloned.1.call-update) | async-done | bytes 1048592 | tf_op jit(solution)/shard_map/all_gather | solution.py:68
  260.5 1.8 multiply_reduce_fusion
  262.4 8.6 %while.43 = (s32[]{:T(128)}, f32[2,512,64]{1,2,0:T(8,128)S(1)}, f32[2,512]{1,0:T(2,128)S(1)}, f32[4096]{0:T(1024)S(1)}, bf16[2,512,128]{2,1,0:T(8,128)(2,1)S(1)}...) while((s32[]{:T(128)}, f32[2,512,64]{1,2,0:T(8,128)S(1)}, ...), condition=%wide.region_12.13_spmd, body=%wide.region_11.12_spmd.sunk | while | flops 815792128 | bytes 2382937 | solution.py:32
  262.4 4.3 %fusion.110 = f32[2,512,64]{1,2,0:T(8,128)S(1)} fusion(f32[2,512,64]{1,2,0:T(8,128)S(1)} %get-tuple-element.405, s32[]{:T(128)} %get-tuple-element.404, bf16[4096,64]{1,0:T(8,128)(2,1)S(1)} %get-tuple-element.418, bf16[4096,128]{1,0:T(8,128)(2,1)} %get-tuple-element.417, f32[4096]{0:T(1024)S(1)} %get-tuple-element.415, f32[512]{0:T(512)S(1)} %bitcast.117, ...), kind=kOutput, calls=%fused_computation.43.clone.1 | convolution fusion | flops 815792128 | bytes 2378752 | tf_op jit(solution)/shard_map/while/body/eval_jaxpr/dot_general | solution.py:30
  266.7 4.3 %fusion.110 = f32[2,512,64]{1,2,0:T(8,128)S(1)} fusion(f32[2,512,64]{1,2,0:T(8,128)S(1)} %get-tuple-element.405, s32[]{:T(128)} %get-tuple-element.404, bf16[4096,64]{1,0:T(8,128)(2,1)S(1)} %get-tuple-element.418, bf16[4096,128]{1,0:T(8,128)(2,1)} %get-tuple-element.417, f32[4096]{0:T(1024)S(1)} %get-tuple-element.415, f32[512]{0:T(512)S(1)} %bitcast.117, ...), kind=kOutput, calls=%fused_computation.43.clone.1 | convolution fusion | flops 815792128 | bytes 2378752 | tf_op jit(solution)/shard_map/while/body/eval_jaxpr/dot_general | solution.py:30
  271.5 80.8 %psum.15 = f32[64,64]{0,1:T(8,128)S(1)} all-reduce(f32[64,64]{0,1:T(8,128)S(1)} %convolution_bitcast_fusion.1), channel_id=1, replica_groups=mesh['group'=8,'leaf'=32] {'group','leaf'}, use_global_device_ids=true, to_apply=%region_13.14 | all-reduce | flops 4096 | bytes 32768 | tf_op jit(solution)/shard_map/psum | solution.py:77
  352.4 5.8 %cholesky.16 = f32[64,64]{1,0:T(8,128)S(1)} custom-call(f32[64,64]{1,0:T(8,128)S(1)} %fusion.54), custom_call_target="Cholesky" | custom-call | tf_op jit(solution)/shard_map/jit(cholesky)/cholesky | solution.py:78
  359.6 4.9 %custom-call.7 = f32[1,64,64]{1,2,0:T(8,128)S(1)} custom-call(f32[1,64,64]{2,1,0:T(8,128)S(1)} %fusion.52), custom_call_target="InvertDiagBlocksLowerTriangular" | custom-call | tf_op jit(solution)/shard_map/jit(_solve_triangular)/triangular_solve | solution.py:79
  364.5 1.1 convolution_multiply_fusion
  (66 shorter events, 11.2 us)
Async XLA Ops:
  7.2 9.7 %copy-start = (bf16[1024,128]{1,0:T(8,128)(2,1)S(1)}, bf16[1024,128]{1,0:T(8,128)(2,1)}, u32[]{:S(2)}) copy-start(bf16[1024,128]{1,0:T(8,128)(2,1)} %param.16) | copy-start | bytes 786436
  7.2 9.4 %copy-start.2 = (bf16[1024,128]{1,0:T(8,128)(2,1)S(1)}, bf16[1024,128]{1,0:T(8,128)(2,1)}, u32[]{:S(2)}) copy-start(bf16[1024,128]{1,0:T(8,128)(2,1)} %param.14) | copy-start | bytes 786436
  7.2 206.3 %all-gather.3.cloned.1.call-start = ((), (), s32[]{:S(2)}) async-start(), calls=%async_computation | async-start | bytes 1081344 | tf_op jit(solution)/shard_map/all_gather | solution.py:51
  8.6 8.2 %copy-start.4 = (bf16[1024,64]{0,1:T(8,128)(2,1)S(1)}, bf16[1024,64]{0,1:T(8,128)(2,1)}, u32[]{:S(2)}) copy-start(bf16[1024,64]{0,1:T(8,128)(2,1)} %param.15) | copy-start | bytes 393220
  11.0 249.5 %all-gather.5.cloned.1.call-start = ((), (), s32[]{:S(2)}) async-start(), calls=%async_computation.1 | async-start | bytes 1179648 | tf_op jit(solution)/shard_map/all_gather | solution.py:68
  12.2 49.4 %copy-start.6 = (bf16[128,512]{1,0:T(8,128)(2,1)S(1)}, bf16[128,512]{1,0:T(8,128)(2,1)}, u32[]{:S(2)}) copy-start(bf16[128,512]{1,0:T(8,128)(2,1)} %param.18) | copy-start | bytes 393220
  13.3 198.5 %collective-permute-start = (bf16[1024,192]{1,0:T(8,128)(2,1)S(1)}, bf16[1024,192]{1,0:T(8,128)(2,1)S(1)}, u32[]{:S(2)}, u32[]{:S(2)}) collective-permute-start(bf16[1024,192]{1,0:T(8,128)(2,1)S(1)} %pad_maximum_fusion), channel_id=1, source_target_pairs={{0,1},{1,0},{2,3},{3,2},{4,5},{5,4},{6,7},{7,6},{8,9},{9,8},{10,11... | collective-permute-start | bytes 1179656 | tf_op jit(solution)/shard_map/ppermute | solution.py:12
  63.5 146.4 %copy-start.7 = (s32[512]{0:T(512)S(1)}, s32[512]{0:T(512)}, u32[]{:S(2)}) copy-start(s32[512]{0:T(512)} %param.19) | copy-start | bytes 6148
  213.5 3.3 copy-start.5
  216.8 3.8 %copy-start.1 = (bf16[4096,128]{1,0:T(8,128)(2,1)S(1)}, bf16[4096,128]{1,0:T(8,128)(2,1)}, u32[]{:S(2)}) copy-start(bf16[4096,128]{1,0:T(8,128)(2,1)} %all-gather.3.cloned.1.call-done) | copy-start | bytes 3145732
  364.5 1.1 copy-start.3
Sparse Core Ops, SparseCore 0:
  11.1 81.7 all-gather.2
  216.9 43.5 all-gather.4
where the time goes:
time: 373 us; the launch traced here: 372 us
  blocking collectives  272 us (73%)
  waiting for transfers between devices  30.7 us (8%)
  matrix products  24.3 us (7%)
  other arithmetic  19.1 us (5%)
  between operations  14.4 us (4%)
  local copies, waits for them, and re-layouts  8.79 us (2%)
    psum x1, blocking collectives, per_device(): weight_whole = lax.psum(weight_term, 'leaf')  123 us
    psum x1, blocking collectives, per_device(): gram_whole = lax.psum(gram_local, ('group', 'leaf'))  80.8 us
    all_gather x1, blocking collectives, per_device(): lax.all_gather(skeleton_weight, 'leaf', axis=0, tiled=True)  44.5 us
    all_gather x1, waiting for transfers between devices, per_device(): key_rows = lax.all_gather(group_points, 'group', axis=0, tiled=True)  30.6 us
    all_gather x1, blocking collectives, per_device(): lax.all_gather(weight_whole.astype(jnp.bfloat16), 'group', axis=0, tiled=...  23.1 us
    dot_general x8, matrix products, one_block(): return jnp.dot(kernel_vals, weights, preferred_element_type=jnp.float32)  22.5 us
  transfers between devices with their start and end apart: 3, of which 1 were waited for; matrix products, arithmetic and copies ran while one was open for 6% of the time, Pallas kernels for 0%

commit v1 on v0

v1 whole, which is shorter than its diff:
```python
import math

import jax
import jax.numpy as jnp
from jax import lax
from jax.experimental import pallas as pl
from jax.experimental.pallas import tpu as pltpu
from jax.sharding import PartitionSpec as P

MESH = pl.DeviceIdType.MESH
F32 = jnp.float32
BF16 = jnp.bfloat16
NX, NYL, NZ, NYH = 4, 2, 8, 2
D = 128
R = 64
N = 1024
KR = 144
BR = KR + R
NEAR = [
    (1, 0), (7, 0), (0, 1), (2, 0), (6, 0), (1, 1), (7, 1), (3, 0),
    (5, 0), (4, 0), (2, 1), (6, 1), (3, 1), (5, 1), (4, 1),
]
FAR = [(dx, dyl, dyh) for dyl in range(2) for dx in (0, 1, 3, 2) if (dx, dyl) != (0, 0) for dyh in range(2)]
PLANE = [(dx, dyl, dyh) for dyl in range(2) for dyh in range(2) for dx in range(4) if (dx, dyl, dyh) != (0, 0, 0)]
NEAR0 = 16
FAR0 = 48
SLOTS = 80


def dot(a, b, ca=1, cb=0, precision=None):
    return lax.dot_general(
        a, b, (((ca,), (cb,)), ((), ())), preferred_element_type=F32, precision=precision
    )


def norm_rows(key_t, as_query):
    keys = key_t.astype(F32)
    norms = jnp.sum(keys * keys, axis=0, keepdims=True) * (-1.0 / 64.0)
    high = norms.astype(BF16).astype(F32)
    rest = norms - high
    mid = rest.astype(BF16).astype(F32)
    low = rest - mid
    row = lax.broadcasted_iota(jnp.int32, (16, key_t.shape[1]), 0)
    if as_query:
        row = jnp.where(row < 6, lax.rem(row + 3, 6), row)
    out = jnp.where(row == 0, high, jnp.where(row == 1, mid, jnp.where(row == 2, low, 0.0)))
    return jnp.where((row >= 3) & (row < 6), 1.0, out).astype(BF16)


def main_kernel(
    pts_hbm, vec_hbm, interp_hbm, lsk_hbm, trans_hbm, gsk_hbm,
    prod_ref, gram_ref,
    pts, vec, interp, lsk, trans, gsk, buf, own, far_own, q, acc,
    gw, gw_in, gp, gp_in, rsw, rsp, wq, pq, g_loc, g_sib, g_z, g_p, g_half,
    load_sem, sib_s, sib_r, near_s, near_r, nyh_s, nfw_s, nfw_r, rs_s, rs_r, zg_s, zg_r,
    far_s, far_r, ffw_s, ffw_r, gz_s, gz_r, gp_s, gp_r,
):
    grp = lax.axis_index("group")
    leaf = lax.axis_index("leaf")
    x, yl = lax.rem(grp, NX), grp // NX
    core, yh, z = lax.rem(leaf, 2), lax.rem(leaf // 2, 2), leaf // 4

    def dev(dx=0, dyl=0, dz=0, dyh=0, dc=0):
        return (
            lax.rem(yl + dyl, NYL) * NX + lax.rem(x + dx, NX),
            lax.rem(z + dz, NZ) * 4 + lax.rem(yh + dyh, 2) * 2 + lax.rem(core + dc, 2),
        )

    def remote(src, dst, ss, rs, to):
        return pltpu.make_async_remote_copy(
            src_ref=src, dst_ref=dst, send_sem=ss, recv_sem=rs, device_id=to, device_id_type=MESH
        )

    loads = [
        pltpu.make_async_copy(s, d, load_sem.at[i])
        for i, (s, d) in enumerate(
            ((pts_hbm, pts), (lsk_hbm, lsk), (vec_hbm, vec), (interp_hbm, interp), (trans_hbm, trans), (gsk_hbm, gsk))
        )
    ]
    for c in loads:
        c.start()
    barrier = pltpu.get_barrier_semaphore()
    peers = [dev(dc=1)]
    peers += [dev(dz=dz, dyh=dyh) for dz, dyh in NEAR]
    peers += [dev(dx=dx, dyl=dyl, dyh=dyh) for dx, dyl, dyh in FAR]
    for p in peers:
        pl.semaphore_signal(barrier, inc=1, device_id=p, device_id_type=MESH)
    sib = dev(dc=1)
    sent = []

    for c in loads:
        c.wait()
    pts_t = jnp.transpose(pts[...])
    hot = (lax.broadcasted_iota(jnp.int32, (N, D), 0) == lsk[...]).astype(F32).astype(BF16)
    skel_t = dot(pts_t, hot).astype(BF16)
    own[0:D, :] = skel_t
    own[D:KR, :] = norm_rows(skel_t, False)
    w_t = dot(vec[...], interp[...])
    own[KR:BR, :] = w_t.astype(BF16)
    w = jnp.transpose(w_t).astype(BF16)
    trans_t = jnp.transpose(trans[...])
    for k in range(4):
        gw[pl.ds(k * 64, 64), 0:R] = dot(trans_t[k * 128 : k * 128 + 64], w)
        gw[pl.ds(k * 64, 64), R : 2 * R] = dot(trans_t[k * 128 + 64 : k * 128 + 128], w)
        pick = lax.broadcasted_iota(jnp.int32, (D, D), 0) + leaf * D == gsk[:, k * D : (k + 1) * D]
        gp[k] = dot(skel_t, pick.astype(F32).astype(BF16)).astype(BF16)
    key_norms = norm_rows(pts_t, False)
    for k in range(8):
        s = slice(k * D, (k + 1) * D)
        buf[k, 0:D, :] = pts_t[:, s]
        buf[k, D:KR, :] = key_norms[:, s]
        buf[k, KR:BR, :] = vec[:, s]
    q[:, 0:D] = pts[...] * jnp.asarray(1.0 / 32.0, BF16)
    q[:, D:KR] = jnp.transpose(norm_rows(pts_t, True))
    acc[...] = jnp.zeros_like(acc)
    for s in (46, 47, 76, 77, 78, 79):
        buf[s] = jnp.zeros((BR, D), BF16)

    pl.semaphore_wait(barrier, len(peers))

    other = 1 - core
    sib_w = remote(gw.at[pl.ds(other * 128, 128)], gw_in, sib_s.at[0], sib_r.at[0], sib)
    sib_p = remote(gp.at[pl.ds(other * 2, 2)], gp_in, sib_s.at[1], sib_r.at[1], sib)
    sib_x = remote(buf.at[pl.ds(0, 8)], buf.at[pl.ds(8, 8)], sib_s.at[2], sib_r.at[2], sib)
    for c in (sib_w, sib_p, sib_x):
        c.start()

    def near_slot(k):
        return buf.at[NEAR0 + 2 * k]

    def near_copy(k):
        dz, dyh = NEAR[k]
        return remote(own, near_slot(k), near_s.at[k], near_r.at[k], dev(dz=dz and NZ - dz, dyh=dyh))

    def near_yh(k):
        dz, _ = NEAR[k]
        j = NEAR.index((dz, 1))
        return remote(near_slot(k), near_slot(j), nyh_s.at[k], near_r.at[j], dev(dyh=1))

    def near_fwd(k):
        return remote(near_slot(k), buf.at[NEAR0 + 2 * k + 1], nfw_s.at[k], nfw_r.at[k], sib)

    def start(make, *args):
        make(*args).start()
        sent.append((make, args))

    def near_arrived(k):
        near_copy(k).wait_recv()
        start(near_fwd, k)
        if NEAR[k][1] == 0:
            start(near_yh, k)

    def rs_to(k):
        dz, dyh = NEAR[k]
        return dev(dz=dz, dyh=dyh), lax.rem(z + dz, NZ), lax.rem(yh + dyh, 2)

    def rs_w(k):
        to, tz, ty = rs_to(k)
        src = gw.at[pl.ds(core * 128 + ty * 64 + tz * 8, 8)]
        return remote(src, rsw.at[k], rs_s.at[0, k], rs_r.at[0, k], to)

    def rs_p(k):
        to, tz, ty = rs_to(k)
        src = gp.at[core * 2 + ty, pl.ds(tz * 16, 16)]
        return remote(src, rsp.at[k], rs_s.at[1, k], rs_r.at[1, k], to)

    def zg_w(d):
        mine = wq.at[pl.ds(z * 8, 8)]
        return remote(mine, mine, zg_s.at[0, d], zg_r.at[0, d], dev(dz=d))

    def zg_p(d):
        mine = pq.at[pl.ds(z * 16, 16)]
        return remote(mine, mine, zg_s.at[1, d], zg_r.at[1, d], dev(dz=d))

    def zg_wait(d):
        fz = lax.rem(z + NZ - d, NZ)
        to = dev(dz=d)
        remote(wq.at[pl.ds(fz * 8, 8)], wq.at[pl.ds(fz * 8, 8)], zg_s.at[0, d], zg_r.at[0, d], to).wait_recv()
        remote(pq.at[pl.ds(fz * 16, 16)], pq.at[pl.ds(fz * 16, 16)], zg_s.at[1, d], zg_r.at[1, d], to).wait_recv()

    def far_copy(k):
        dx, dyl, dyh = FAR[k]
        return remote(
            far_own, buf.at[FAR0 + 2 * k], far_s.at[k], far_r.at[k],
            dev(dx=dx and NX - dx, dyl=dyl, dyh=dyh),
        )

    def far_fwd(k):
        return remote(buf.at[FAR0 + 2 * k], buf.at[FAR0 + 2 * k + 1], ffw_s.at[k], ffw_r.at[k], sib)

    def phase_sib():
        sib_w.wait_recv()
        sib_p.wait_recv()
        mine = pl.ds(core * 128, 128)
        gw[mine] = gw[mine] + gw_in[...]
        mine = pl.ds(core * 2, 2)
        gp[mine] = gp[mine] + gp_in[...]
        for k in range(15):
            start(rs_w, k)
            start(rs_p, k)
        for k in range(15):
            if NEAR[k][1] == 0 or NEAR[k][0] == 0:
                start(near_copy, k)
        sib_x.wait_recv()

    def phase_near0():
        for k in (0, 1, 2, 3, 4):
            near_arrived(k)
        for k in (0, 1, 2, 3):
            near_fwd(k).wait_recv()

    def phase_rs():
        for k in range(15):
            rs_w(k).wait_recv()
            rs_p(k).wait_recv()
        total = gw[pl.ds(core * 128 + yh * 64 + z * 8, 8)]
        rows = gp[core * 2 + yh, pl.ds(z * 16, 16)].astype(F32)
        for k in range(15):
            total = total + rsw[k]
            rows = rows + rsp[k].astype(F32)
        wq[pl.ds(z * 8, 8)] = total
        pq[pl.ds(z * 16, 16)] = rows.astype(BF16)
        for d in range(1, 8):
            start(zg_w, d)
            start(zg_p, d)
        for k in (7, 8, 5, 6):
            near_arrived(k)
        for k in (4, 5, 6, 7):
            near_fwd(k).wait_recv()

    def phase_near2():
        for k in (9, 10, 11):
            near_arrived(k)
        for k in (8, 9, 10, 11):
            near_fwd(k).wait_recv()

    def phase_zg():
        for d in range(1, 8):
            zg_wait(d)
        pq_v = pq[...]
        far_own[0:D, :] = pq_v
        far_own[D:KR, :] = norm_rows(pq_v, False)
        wq_t = jnp.transpose(wq[...])
        far_own[KR:BR, :] = jnp.concatenate([wq_t[0:R], wq_t[R : 2 * R]], axis=1).astype(BF16)
        for k in range(14):
            start(far_copy, k)
        for k in (12, 13, 14):
            near_arrived(k)
        for k in (12, 13, 14):
            near_fwd(k).wait_recv()

    def phase_far(lo, hi):
        def run():
            for k in range(lo, hi):
                far_copy(k).wait_recv()
                start(far_fwd, k)
            for k in range(lo, hi):
                far_fwd(k).wait_recv()

        return run

    phases = {
        1: phase_sib,
        2: phase_near0,
        3: phase_rs,
        4: phase_near2,
        5: phase_zg,
        6: phase_far(0, 4),
        7: phase_far(4, 8),
        8: phase_far(8, 12),
        9: phase_far(12, 14),
    }

    def chunk(i, carry):
        for n, phase in phases.items():
            pl.when(i == n)(phase)
        base = i * 8
        keys = jnp.concatenate([buf[base + j, 0:KR, :] for j in range(8)], axis=1)
        weights = jnp.concatenate([buf[base + j, KR:BR, :] for j in range(8)], axis=1)
        for t in range(4):
            rows = pl.ds(t * 256, 256)
            kernel_vals = jnp.exp(dot(q[rows, :], keys)).astype(BF16)
            acc[rows, :] += dot(kernel_vals, weights, 1, 1)
        return carry

    lax.fori_loop(0, 10, chunk, 0)

    prod_t = jnp.transpose(acc[...])
    prod_ref[...] = prod_t
    gram = dot(prod_t, acc[...], precision=lax.Precision.HIGHEST)
    g_loc[...] = jnp.concatenate([gram[0:32], gram[32:64]], axis=1)
    def gram_sib():
        return remote(g_loc.at[pl.ds(other * 16, 16)], g_sib, sib_s.at[3], sib_r.at[3], sib)

    def gram_z(d):
        return remote(g_z.at[z], g_z.at[z], gz_s.at[d], gz_r.at[d], dev(dz=d))

    def gram_plane(k):
        dx, dyl, dyh = PLANE[k]
        return remote(g_p.at[here], g_p.at[here], gp_s.at[k], gp_r.at[k], dev(dx=dx, dyl=dyl, dyh=dyh))

    def gram_back():
        mine = g_half.at[pl.ds(core * 16, 16)]
        return remote(mine, mine, sib_s.at[4], sib_r.at[4], sib)

    start(gram_sib)
    gram_sib().wait_recv()
    g_z[z] = g_loc[pl.ds(core * 16, 16)] + g_sib[...]
    for d in range(1, 8):
        start(gram_z, d)
    for d in range(1, 8):
        fz = lax.rem(z + NZ - d, NZ)
        remote(g_z.at[fz], g_z.at[fz], gz_s.at[d], gz_r.at[d], dev(dz=d)).wait_recv()
    total = g_z[0]
    for k in range(1, 8):
        total = total + g_z[k]
    here = (yl * 2 + yh) * 4 + x
    g_p[here] = total
    for k in range(15):
        start(gram_plane, k)
    for k, (dx, dyl, dyh) in enumerate(PLANE):
        there = (lax.rem(yl + dyl, 2) * 2 + lax.rem(yh + dyh, 2)) * 4 + lax.rem(x + NX - dx, NX)
        remote(
            g_p.at[there], g_p.at[there], gp_s.at[k], gp_r.at[k], dev(dx=dx, dyl=dyl, dyh=dyh)
        ).wait_recv()
    total = g_p[0]
    for k in range(1, 16):
        total = total + g_p[k]
    g_half[pl.ds(core * 16, 16)] = total
    start(gram_back)
    theirs = g_half.at[pl.ds(other * 16, 16)]
    remote(theirs, theirs, sib_s.at[4], sib_r.at[4], sib).wait_recv()
    gram_ref[...] = g_half[...]
    for c in (sib_w, sib_p, sib_x):
        c.wait_send()
    for make, args in sent:
        make(*args).wait_send()


def tail_kernel(prod_ref, gram_ref, out_ref, basis_ref, work):
    packed = gram_ref[...]
    gram = jnp.concatenate([packed[:, 0:R], packed[:, R : 2 * R]], axis=0)
    row = lax.broadcasted_iota(jnp.int32, (R, 2 * R), 0)
    lane = lax.broadcasted_iota(jnp.int32, (R, 2 * R), 1)
    work[...] = jnp.concatenate([gram, (row == lane).astype(F32)[:, 0:R]], axis=1)
    out_ref[...] = prod_ref[...]

    def step(k, scale):
        a = work[...]
        pivot = work[pl.ds(k, 1), :]
        col = jnp.sum(jnp.where(lane == k, a, 0.0), axis=1, keepdims=True)
        diag = jnp.sum(jnp.where(lane[0:1] == k, pivot, 0.0), axis=1, keepdims=True)
        factor = jnp.where(row[:, 0:1] > k, col / diag, 0.0)
        work[...] = a - factor * pivot
        return jnp.where(row[:, 0:1] == k, lax.rsqrt(diag), scale)

    scale = lax.fori_loop(0, R, step, jnp.zeros((R, 1), F32))
    inverse = work[:, R : 2 * R] * (scale * 512.0)
    basis_ref[...] = dot(inverse, prod_ref[...], precision=lax.Precision.HIGHEST)


def per_device(points, vectors, leaf_interp, leaf_skeleton, group_transfer, group_skeleton):
    hbm = pl.BlockSpec(memory_space=pl.ANY)
    vmem = pl.BlockSpec(memory_space=pltpu.VMEM)
    dma = pltpu.SemaphoreType.DMA
    prod_t, gram = pl.pallas_call(
        main_kernel,
        out_shape=(jax.ShapeDtypeStruct((R, N), F32), jax.ShapeDtypeStruct((32, 128), F32)),
        in_specs=[hbm] * 6,
        out_specs=(vmem, vmem),
        scratch_shapes=[
            pltpu.VMEM((N, D), BF16),
            pltpu.VMEM((R, N), BF16),
            pltpu.VMEM((N, D), BF16),
            pltpu.VMEM((1, 128), jnp.int32),
            pltpu.VMEM((128, 512), BF16),
            pltpu.VMEM((1, 512), jnp.int32),
            pltpu.VMEM((SLOTS, BR, D), BF16),
            pltpu.VMEM((BR, D), BF16),
            pltpu.VMEM((BR, D), BF16),
            pltpu.VMEM((N, KR), BF16),
            pltpu.VMEM((N, R), F32),
            pltpu.VMEM((256, 128), F32),
            pltpu.VMEM((128, 128), F32),
            pltpu.VMEM((4, 128, 128), BF16),
            pltpu.VMEM((2, 128, 128), BF16),
            pltpu.VMEM((15, 8, 128), F32),
            pltpu.VMEM((15, 16, 128), BF16),
            pltpu.VMEM((64, 128), F32),
            pltpu.VMEM((128, 128), BF16),
            pltpu.VMEM((32, 128), F32),
            pltpu.VMEM((16, 128), F32),
            pltpu.VMEM((8, 16, 128), F32),
            pltpu.VMEM((16, 16, 128), F32),
            pltpu.VMEM((32, 128), F32),
            dma((6,)),
            dma((5,)),
            dma((5,)),
            dma((15,)),
            dma((15,)),
            dma((15,)),
            dma((15,)),
            dma((15,)),
            dma((2, 15)),
            dma((2, 15)),
            dma((2, 8)),
            dma((2, 8)),
            dma((14,)),
            dma((14,)),
            dma((14,)),
            dma((14,)),
            dma((8,)),
            dma((8,)),
            dma((15,)),
            dma((15,)),
        ],
        compiler_params=pltpu.CompilerParams(
            collective_id=0, has_side_effects=True, vmem_limit_bytes=40 * 2**20
        ),
        name="hss_main",
    )(
        points,
        vectors.T,
        leaf_interp,
        leaf_skeleton.reshape(1, 128),
        group_transfer,
        group_skeleton.reshape(1, 512),
    )
    out_t, basis_t = pl.pallas_call(
        tail_kernel,
        out_shape=(jax.ShapeDtypeStruct((R, N), F32), jax.ShapeDtypeStruct((R, N), F32)),
        in_specs=[vmem, vmem],
        out_specs=(vmem, vmem),
        scratch_shapes=[pltpu.VMEM((R, 2 * R), F32)],
        compiler_params=pltpu.CompilerParams(vmem_limit_bytes=16 * 2**20),
        name="hss_tail",
    )(prod_t, gram)
    return out_t.T, basis_t.T


def solution(mesh):
    spec = P(("group", "leaf"), None)
    return jax.shard_map(
        per_device,
        mesh=mesh,
        in_specs=(spec, spec, spec, P(("group", "leaf")), spec, P("group")),
        out_specs=(spec, spec),
        check_vma=False,
    )
```

time: 373 us -> 78.3 us (0.21)
  blocking collectives: 272 us -> 0 us
  Pallas kernels: 0 us -> 73.1 us
  waiting for transfers between devices: 30.7 us -> 0 us
  matrix products: 24.3 us -> 0 us
  other arithmetic: 19.1 us -> 0 us
  between operations: 14.4 us -> 0.66 us
  local copies, waits for them, and re-layouts: 8.79 us -> 4.38 us
    psum x2 -> x0, blocking collectives: 204 us -> none  [the longest x1 123 us: per_device(): weight_whole = lax.psum(weight_term, 'leaf')]
    pallas_call x0 -> x2, Pallas kernels: none -> 73.1 us  [the longest x1 65.7 us: per_device(): pl.pallas_call(main_kernel, out_shape=(jax.ShapeDtypeStruct((R, N), F32),...]
    all_gather x2 -> x0, blocking collectives: 67.6 us -> none  [the longest x1 44.5 us: per_device(): lax.all_gather(skeleton_weight, 'leaf', axis=0, tiled=True)]
    all_gather x2 -> x0, waiting for transfers between devices: 30.7 us -> none  [the longest x1 30.6 us: per_device(): key_rows = lax.all_gather(group_points, 'group', axis=0, tiled=True)]
    dot_general x11 -> x0, matrix products: 23.2 us -> none  [the longest x8 22.5 us: one_block(): return jnp.dot(kernel_vals, weights, preferred_element_type=jnp.float32)]
    another operation x5 -> x0, other arithmetic: 12.1 us -> none  [the longest x3 6.52 us: per_device(): lower = jnp.linalg.cholesky(gram_whole)]
    gather x2 -> x0, local copies, waits for them, and re-layouts: 4.12 us -> none  [the longest x1 2.45 us: per_device(): group_points = jnp.take(gathered_points, group_skeleton, axis=0)]
  transfers between devices with their start and end apart: 3 -> 0, of which waited for: 1 -> 0; matrix products, arithmetic and copies ran while one was open for 6% -> 0% of each run, Pallas kernels for 0% -> 0%
where the time goes in v1:
time: 78.3 us; the launch traced here: 78.1 us
  Pallas kernels  73.1 us (93%)
  local copies, waits for them, and re-layouts  4.38 us (6%)
    pallas_call x1, Pallas kernels, per_device(): pl.pallas_call(main_kernel, out_shape=(jax.ShapeDtypeStruct((R, N), F32),...  65.7 us
    pallas_call x1, Pallas kernels, per_device(): pl.pallas_call(tail_kernel, out_shape=(jax.ShapeDtypeStruct((R, N), F32),...  7.44 us
    unnamed x12, local copies, waits for them, and re-layouts  4.38 us

profile of v1, /device:TPU:1, one launch (start us, length us, event | category | flops | bytes accessed | tf_op | source)
XLA Modules:
  0.0 78.1 jit_solution(5944280735705767973)
XLA Ops:
  0.6 0.0 copy-start.4
  0.6 0.0 copy-start.5
  0.7 0.7 copy-done.4
  1.3 0.0 copy-done.5
  1.3 0.0 copy-start
  1.3 0.9 %copy-done = bf16[1024,128]{1,0:T(8,128)(2,1)S(1)} copy-done((bf16[1024,128]{1,0:T(8,128)(2,1)S(1)}, bf16[1024,128]{1,0:T(8,128)(2,1)}, u32[]{:S(2)}) %copy-start) | copy-done | bytes 262168
  2.3 0.0 copy-start.1
  2.3 0.9 %copy-done.1 = bf16[1024,128]{1,0:T(8,128)(2,1)S(1)} copy-done((bf16[1024,128]{1,0:T(8,128)(2,1)S(1)}, bf16[1024,128]{1,0:T(8,128)(2,1)}, u32[]{:S(2)}) %copy-start.1) | copy-done | bytes 262168
  3.2 0.0 copy-start.2
  3.2 0.9 %copy-done.2 = bf16[1024,64]{0,1:T(8,128)(2,1)S(1)} copy-done((bf16[1024,64]{0,1:T(8,128)(2,1)S(1)}, bf16[1024,64]{0,1:T(8,128)(2,1)}, u32[]{:S(2)}) %copy-start.2) | copy-done | bytes 131096
  4.1 0.0 copy-start.3
  4.1 0.9 %copy-done.3 = bf16[128,512]{1,0:T(8,128)(2,1)S(1)} copy-done((bf16[128,512]{1,0:T(8,128)(2,1)S(1)}, bf16[128,512]{1,0:T(8,128)(2,1)}, u32[]{:S(2)}) %copy-start.3) | copy-done | bytes 131096
  5.0 65.7 %hss_main.1 = (f32[64,1024]{1,0:T(8,128)S(1)}, f32[32,128]{1,0:T(8,128)S(1)}) custom-call(bf16[1024,128]{1,0:T(8,128)(2,1)S(1)} %copy-done, bf16[64,1024]{1,0:T(8,128)(2,1)S(1)} %bitcast.5, bf16[1024,128]{1,0:T(8,128)(2,1)S(1)} %copy-done.1, s32[1,128]{1,0:T(1,128)S(1)} %bitcast.7, bf16[128,512]{1,0:T(8,128)(2,1)S(1)} %copy-done.3, s32[1,512]{1,0:T(1,128)S(1)} %bitcast.6), custom_call_target="tpu_custom_call" | custom-call | tf_op jit(solution)/shard_map/hss_main/pallas_call | solution.py:366
  70.7 7.4 %hss_tail.1 = (f32[64,1024]{1,0:T(8,128)}, f32[64,1024]{1,0:T(8,128)}) custom-call(f32[64,1024]{1,0:T(8,128)S(1)} %get-tuple-element.6.prod_ref, f32[32,128]{1,0:T(8,128)S(1)} %get-tuple-element.7.gram_ref), custom_call_target="tpu_custom_call" | custom-call | tf_op jit(solution)/shard_map/hss_tail/pallas_call | solution.py:429
Async XLA Ops:
  0.6 0.7 copy-start.4
  0.6 0.7 copy-start.5
  1.3 1.0 %copy-start = (bf16[1024,128]{1,0:T(8,128)(2,1)S(1)}, bf16[1024,128]{1,0:T(8,128)(2,1)}, u32[]{:S(2)}) copy-start(bf16[1024,128]{1,0:T(8,128)(2,1)} %pts_hbm.1) | copy-start | bytes 786436
  2.3 0.9 %copy-start.1 = (bf16[1024,128]{1,0:T(8,128)(2,1)S(1)}, bf16[1024,128]{1,0:T(8,128)(2,1)}, u32[]{:S(2)}) copy-start(bf16[1024,128]{1,0:T(8,128)(2,1)} %interp_hbm.1) | copy-start | bytes 786436
  3.2 0.9 %copy-start.2 = (bf16[1024,64]{0,1:T(8,128)(2,1)S(1)}, bf16[1024,64]{0,1:T(8,128)(2,1)}, u32[]{:S(2)}) copy-start(bf16[1024,64]{0,1:T(8,128)(2,1)} %param.7) | copy-start | bytes 393220
  4.1 0.9 %copy-start.3 = (bf16[128,512]{1,0:T(8,128)(2,1)S(1)}, bf16[128,512]{1,0:T(8,128)(2,1)}, u32[]{:S(2)}) copy-start(bf16[128,512]{1,0:T(8,128)(2,1)} %trans_hbm.1) | copy-start | bytes 393220

commit v2 on v1

v2 whole, which is shorter than its diff:
```python
import math

import jax
import jax.numpy as jnp
from jax import lax
from jax.experimental import pallas as pl
from jax.experimental.pallas import tpu as pltpu
from jax.sharding import PartitionSpec as P

MESH = pl.DeviceIdType.MESH
F32 = jnp.float32
BF16 = jnp.bfloat16
NX, NYL, NZ, NYH = 4, 2, 8, 2
D = 128
R = 64
N = 1024
KR = 144
BR = KR + R
NEAR = [
    (1, 0), (7, 0), (0, 1), (2, 0), (6, 0), (1, 1), (7, 1), (3, 0),
    (5, 0), (4, 0), (2, 1), (6, 1), (3, 1), (5, 1), (4, 1),
]
FAR = [
    ("y", 0, 1), ("y", 0, 3), ("x", 1, 0), ("x", 1, 1), ("x", 3, 0), ("x", 3, 1), ("y", 1, 1),
    ("y", 1, 3), ("y", 3, 1), ("y", 3, 3), ("x", 2, 0), ("x", 2, 1), ("y", 2, 1), ("y", 2, 3),
]
PLANE = [(dx, dyl, dyh) for dyl in range(2) for dyh in range(2) for dx in range(4) if (dx, dyl, dyh) != (0, 0, 0)]
NEAR0 = 16
FAR0 = 48
SLOTS = 80


def dot(a, b, ca=1, cb=0, precision=None):
    return lax.dot_general(
        a, b, (((ca,), (cb,)), ((), ())), preferred_element_type=F32, precision=precision
    )


def norm_rows(key_t, as_query):
    keys = key_t.astype(F32)
    norms = jnp.sum(keys * keys, axis=0, keepdims=True) * (-1.0 / 64.0)
    high = norms.astype(BF16).astype(F32)
    rest = norms - high
    mid = rest.astype(BF16).astype(F32)
    low = rest - mid
    row = lax.broadcasted_iota(jnp.int32, (16, key_t.shape[1]), 0)
    if as_query:
        row = jnp.where(row < 6, lax.rem(row + 3, 6), row)
    out = jnp.where(row == 0, high, jnp.where(row == 1, mid, jnp.where(row == 2, low, 0.0)))
    return jnp.where((row >= 3) & (row < 6), 1.0, out).astype(BF16)


def main_kernel(
    pts_hbm, vec_hbm, interp_hbm, lsk_hbm, trans_hbm, gsk_hbm,
    prod_ref, gram_ref,
    pts, vec, interp, lsk, trans, gsk, buf, own, far_own, q, acc,
    gw, gw_in, gp, gp_in, rsw, rsp, pair_in_w, pair_in_p, ag, g_loc, g_sib, g_z, g_p, g_half,
    load_sem, sib_s, sib_r, near_s, near_r, nyh_s, nfw_s, nfw_r, rs_s, rs_r, zg_s, zg_r,
    far_s, far_r, ffw_s, ffw_r, gz_s, gz_r, gp_s, gp_r,
):
    grp = lax.axis_index("group")
    leaf = lax.axis_index("leaf")
    x, yl = lax.rem(grp, NX), grp // NX
    core, yh, z = lax.rem(leaf, 2), lax.rem(leaf // 2, 2), leaf // 4

    def dev(dx=0, dyl=0, dz=0, dyh=0, dc=0):
        return (
            lax.rem(yl + dyl, NYL) * NX + lax.rem(x + dx, NX),
            lax.rem(z + dz, NZ) * 4 + lax.rem(yh + dyh, 2) * 2 + lax.rem(core + dc, 2),
        )

    def ydev(dy):
        y = lax.rem(yh * 2 + yl + dy, 4)
        return (lax.rem(y, 2) * NX + x, z * 4 + (y // 2) * 2 + core)

    def remote(src, dst, ss, rs, to):
        return pltpu.make_async_remote_copy(
            src_ref=src, dst_ref=dst, send_sem=ss, recv_sem=rs, device_id=to, device_id_type=MESH
        )

    loads = [
        pltpu.make_async_copy(s, d, load_sem.at[i])
        for i, (s, d) in enumerate(
            ((pts_hbm, pts), (lsk_hbm, lsk), (vec_hbm, vec), (interp_hbm, interp), (trans_hbm, trans), (gsk_hbm, gsk))
        )
    ]
    for c in loads:
        c.start()
    barrier = pltpu.get_barrier_semaphore()
    peers = [dev(dc=1)]
    peers += [dev(dz=d) for d in range(1, 8)] + [dev(dyh=1)]
    peers += [dev(dx=dx) for dx in (1, 2, 3)] + [ydev(1), ydev(3)]
    for p in peers:
        pl.semaphore_signal(barrier, inc=1, device_id=p, device_id_type=MESH)
    sib = dev(dc=1)
    sent = []

    for c in loads:
        c.wait()
    pts_t = jnp.transpose(pts[...])
    hot = (lax.broadcasted_iota(jnp.int32, (N, D), 0) == lsk[...]).astype(F32).astype(BF16)
    skel_t = dot(pts_t, hot).astype(BF16)
    own[0:D, :] = skel_t
    own[D:KR, :] = norm_rows(skel_t, False)
    w_t = dot(vec[...], interp[...])
    own[KR:BR, :] = w_t.astype(BF16)
    w = jnp.transpose(w_t).astype(BF16)
    trans_t = jnp.transpose(trans[...])
    for k in range(4):
        half, n = k // 2, k % 2
        left = dot(trans_t[k * 128 : k * 128 + 64], w)
        right = dot(trans_t[k * 128 + 64 : k * 128 + 128], w)
        pick = lax.broadcasted_iota(jnp.int32, (D, D), 0) + leaf * D == gsk[:, k * D : (k + 1) * D]
        picked = dot(skel_t, pick.astype(F32).astype(BF16)).astype(BF16)
        for t in range(NZ):
            gw[half, t, n * 8 : n * 8 + 8, 0:R] = left[t * 8 : t * 8 + 8]
            gw[half, t, n * 8 : n * 8 + 8, R : 2 * R] = right[t * 8 : t * 8 + 8]
            gp[half, t, n * 16 : n * 16 + 16, :] = picked[t * 16 : t * 16 + 16]
    key_norms = norm_rows(pts_t, False)
    for k in range(8):
        s = slice(k * D, (k + 1) * D)
        buf[k, 0:D, :] = pts_t[:, s]
        buf[k, D:KR, :] = key_norms[:, s]
        buf[k, KR:BR, :] = vec[:, s]
    q[:, 0:D] = pts[...] * jnp.asarray(1.0 / 32.0, BF16)
    q[:, D:KR] = jnp.transpose(norm_rows(pts_t, True))
    acc[...] = jnp.zeros_like(acc)
    for s in (46, 47, 76, 77, 78, 79):
        buf[s] = jnp.zeros((BR, D), BF16)

    pl.semaphore_wait(barrier, len(peers))

    other = 1 - core
    sib_w = remote(gw.at[other], gw_in, sib_s.at[0], sib_r.at[0], sib)
    sib_p = remote(gp.at[other], gp_in, sib_s.at[1], sib_r.at[1], sib)
    sib_x = remote(buf.at[pl.ds(0, 8)], buf.at[pl.ds(8, 8)], sib_s.at[2], sib_r.at[2], sib)
    for c in (sib_w, sib_p, sib_x):
        c.start()

    def near_slot(k):
        return buf.at[NEAR0 + 2 * k]

    def near_copy(k):
        dz, dyh = NEAR[k]
        return remote(own, near_slot(k), near_s.at[k], near_r.at[k], dev(dz=dz and NZ - dz, dyh=dyh))

    def near_yh(k):
        dz, _ = NEAR[k]
        j = NEAR.index((dz, 1))
        return remote(near_slot(k), near_slot(j), nyh_s.at[k], near_r.at[j], dev(dyh=1))

    def near_fwd(k):
        return remote(near_slot(k), buf.at[NEAR0 + 2 * k + 1], nfw_s.at[k], nfw_r.at[k], sib)

    def start(make, *args):
        make(*args).start()
        sent.append((make, args))

    def near_arrived(k):
        near_copy(k).wait_recv()
        start(near_fwd, k)
        if NEAR[k][1] == 0:
            start(near_yh, k)

    def rs_w(d):
        return remote(gw.at[core, lax.rem(z + d, NZ)], rsw.at[d], rs_s.at[0, d], rs_r.at[0, d], dev(dz=d))

    def rs_p(d):
        return remote(gp.at[core, lax.rem(z + d, NZ)], rsp.at[d], rs_s.at[1, d], rs_r.at[1, d], dev(dz=d))

    def pair_w():
        return remote(rsw.at[0], pair_in_w, sib_s.at[5], sib_r.at[5], dev(dyh=1))

    def pair_p():
        return remote(rsp.at[0], pair_in_p, sib_s.at[6], sib_r.at[6], dev(dyh=1))

    def zg(d):
        return remote(ag.at[z], ag.at[z], zg_s.at[d], zg_r.at[d], dev(dz=d))

    def zg_wait(d):
        theirs = ag.at[lax.rem(z + NZ - d, NZ)]
        remote(theirs, theirs, zg_s.at[d], zg_r.at[d], dev(dz=d)).wait_recv()

    def far_slot(k):
        return buf.at[FAR0 + 2 * k]

    def far_copy(k):
        axis, dx, n = FAR[k]
        if axis == "x":
            return remote(far_own.at[n], far_slot(k), far_s.at[k], far_r.at[k], dev(dx=NX - dx))
        quarter = 0 if n == 3 else 1
        src = far_own.at[quarter] if dx == 0 else far_slot(FAR.index(("x", dx, quarter)))
        return remote(src, far_slot(k), far_s.at[k], far_r.at[k], ydev(4 - n))

    def far_fwd(k):
        return remote(buf.at[FAR0 + 2 * k], buf.at[FAR0 + 2 * k + 1], ffw_s.at[k], ffw_r.at[k], sib)

    def phase_start():
        sib_w.wait_recv()
        sib_p.wait_recv()
        gw[core] = gw[core] + gw_in[...]
        gp[core] = gp[core] + gp_in[...]
        for d in range(1, 8):
            start(rs_w, d)
            start(rs_p, d)
        for k in (0, 1, 2, 3, 4):
            start(near_copy, k)

    def phase_sib():
        sib_x.wait_recv()

    def phase_rs():
        for d in range(1, 8):
            rs_w(d).wait_recv()
            rs_p(d).wait_recv()
        total = gw[core, z]
        rows = gp[core, z].astype(F32)
        for d in range(1, 8):
            total = total + rsw[d]
            rows = rows + rsp[d].astype(F32)
        rsw[0] = total
        rsp[0] = rows.astype(BF16)
        start(pair_w)
        start(pair_p)
        for k in (7, 8, 9):
            start(near_copy, k)

    def phase_pair():
        pair_w().wait_recv()
        pair_p().wait_recv()
        ag[z, 0:16, :] = (rsw[0] + pair_in_w[...]).astype(BF16)
        ag[z, 16:48, :] = rsp[0] + pair_in_p[...]
        for d in range(1, 8):
            start(zg, d)

    def near_phase(arrive, use):
        for k in arrive:
            near_arrived(k)
        for k in use:
            near_fwd(k).wait_recv()

    def phase_near0():
        near_phase((0, 1, 2, 3, 4), (0, 1, 2, 3))

    def phase_near1():
        near_phase((7, 8, 9, 5, 6), (4, 5, 6, 7))

    def phase_near2():
        near_phase((10, 11), (8, 9, 10, 11))

    def phase_near3():
        near_phase((12, 13, 14), (12, 13, 14))

    def phase_zg():
        for d in range(1, 8):
            zg_wait(d)
        for n in range(2):
            points_t = jnp.concatenate([ag[t, 16 + n * 16 : 32 + n * 16, :] for t in range(NZ)], axis=0)
            far_own[n, 0:D, :] = points_t
            far_own[n, D:KR, :] = norm_rows(points_t, False)
            pairs = jnp.concatenate(
                [ag[t, 0:16, :].astype(F32)[n * 8 : n * 8 + 8] for t in range(NZ)], axis=0
            )
            w_pairs = jnp.transpose(pairs)
            far_own[n, KR:BR, :] = jnp.concatenate([w_pairs[0:R], w_pairs[R : 2 * R]], axis=1).astype(BF16)
        for k, (axis, dx, _) in enumerate(FAR):
            if axis == "x" or dx == 0:
                start(far_copy, k)

    def phase_far(arrive, use):
        def far():
            for k in arrive:
                far_copy(k).wait_recv()
                start(far_fwd, k)
                axis, dx, n = FAR[k]
                if axis == "x":
                    start(far_copy, FAR.index(("y", dx, 3 if n == 0 else 1)))
            for k in use:
                far_fwd(k).wait_recv()

        return far

    with jax.named_scope("phase_start"):
        phase_start()
    phases = [
        (1, phase_sib),
        (2, phase_rs),
        (2, phase_near0),
        (3, phase_pair),
        (3, phase_near1),
        (4, phase_zg),
        (4, phase_near2),
        (5, phase_near3),
        (6, phase_far((0, 1, 2, 3, 4, 5), (0, 1, 2, 3))),
        (7, phase_far((10, 11, 6, 7), (4, 5, 6, 7))),
        (8, phase_far((8, 9), (8, 9, 10, 11))),
        (9, phase_far((12, 13), (12, 13))),
    ]

    def chunk(i, carry):
        for n, phase in phases:
            with jax.named_scope(phase.__name__):
                pl.when(i == n)(phase)
        base = i * 8
        keys = jnp.concatenate([buf[base + j, 0:KR, :] for j in range(8)], axis=1)
        weights = jnp.concatenate([buf[base + j, KR:BR, :] for j in range(8)], axis=1)
        for t in range(4):
            rows = pl.ds(t * 256, 256)
            kernel_vals = jnp.exp(dot(q[rows, :], keys)).astype(BF16)
            acc[rows, :] += dot(kernel_vals, weights, 1, 1)
        return carry

    lax.fori_loop(0, 10, chunk, 0)

    prod_t = jnp.transpose(acc[...])
    prod_ref[...] = prod_t
    gram = dot(prod_t, acc[...], precision=lax.Precision.HIGHEST)
    g_loc[...] = jnp.concatenate([gram[0:32], gram[32:64]], axis=1)
    def gram_sib():
        return remote(g_loc.at[pl.ds(other * 16, 16)], g_sib, sib_s.at[3], sib_r.at[3], sib)

    def gram_z(d):
        return remote(g_z.at[z], g_z.at[z], gz_s.at[d], gz_r.at[d], dev(dz=d))

    def gram_plane(k):
        dx, dyl, dyh = PLANE[k]
        return remote(g_p.at[here], g_p.at[here], gp_s.at[k], gp_r.at[k], dev(dx=dx, dyl=dyl, dyh=dyh))

    def gram_back():
        mine = g_half.at[pl.ds(core * 16, 16)]
        return remote(mine, mine, sib_s.at[4], sib_r.at[4], sib)

    start(gram_sib)
    gram_sib().wait_recv()
    g_z[z] = g_loc[pl.ds(core * 16, 16)] + g_sib[...]
    for d in range(1, 8):
        start(gram_z, d)
    for d in range(1, 8):
        fz = lax.rem(z + NZ - d, NZ)
        remote(g_z.at[fz], g_z.at[fz], gz_s.at[d], gz_r.at[d], dev(dz=d)).wait_recv()
    total = g_z[0]
    for k in range(1, 8):
        total = total + g_z[k]
    here = (yl * 2 + yh) * 4 + x
    g_p[here] = total
    for k in range(15):
        start(gram_plane, k)
    for k, (dx, dyl, dyh) in enumerate(PLANE):
        there = (lax.rem(yl + dyl, 2) * 2 + lax.rem(yh + dyh, 2)) * 4 + lax.rem(x + NX - dx, NX)
        remote(
            g_p.at[there], g_p.at[there], gp_s.at[k], gp_r.at[k], dev(dx=dx, dyl=dyl, dyh=dyh)
        ).wait_recv()
    total = g_p[0]
    for k in range(1, 16):
        total = total + g_p[k]
    g_half[pl.ds(core * 16, 16)] = total
    start(gram_back)
    theirs = g_half.at[pl.ds(other * 16, 16)]
    remote(theirs, theirs, sib_s.at[4], sib_r.at[4], sib).wait_recv()
    gram_ref[...] = g_half[...]
    for c in (sib_w, sib_p, sib_x):
        c.wait_send()
    for make, args in sent:
        make(*args).wait_send()


def split(v):
    high = v.astype(BF16)
    return high, (v - high.astype(F32)).astype(BF16)


def wide(v):
    return jnp.broadcast_to(v, (8, 128))


def tail_kernel(prod_ref, gram_ref, out_hbm, basis_ref, sem):
    copy = pltpu.make_async_copy(prod_ref, out_hbm, sem)
    copy.start()
    packed = gram_ref[...]
    gram = jnp.concatenate([packed[:, 0:R], packed[:, R : 2 * R]], axis=0)
    row = lax.broadcasted_iota(jnp.int32, (R, R), 0)
    lane = lax.broadcasted_iota(jnp.int32, (R, R), 1)
    full = jnp.concatenate([gram, (row == lane).astype(F32)], axis=1)
    rows = [full[8 * i : 8 * i + 8, :] for i in range(8)]
    sub = lax.broadcasted_iota(jnp.int32, (8, 128), 0)
    for b in range(8):
        col = {(j, i): wide(rows[i][:, 8 * b + j : 8 * b + j + 1]) for j in range(8) for i in range(b, 8)}
        diag = jnp.zeros((8, 128), F32)
        for j in range(8):
            d = wide(col[j, b][j : j + 1, :])
            inv = 1.0 / d
            diag = jnp.where(sub == j, d, diag)
            pivot = wide(rows[b][j : j + 1, :])
            heads = {n: wide(col[n, b][j : j + 1, :]) for n in range(j + 1, 8)}
            for i in range(b, 8):
                m = col[j, i] * inv
                if i == b:
                    m = jnp.where(sub > j, m, 0.0)
                rows[i] = rows[i] - m * pivot
                for n in range(j + 1, 8):
                    col[n, i] = col[n, i] - m * heads[n]
        rows[b] = rows[b] * (lax.rsqrt(diag) * 512.0)
    inverse = jnp.concatenate(rows, axis=0)[:, R : 2 * R]
    lh, ll = split(inverse)
    xh, xl = split(prod_ref[...])
    basis_ref[...] = dot(
        jnp.concatenate([lh, lh, ll], axis=1), jnp.concatenate([xh, xl, xh], axis=0)
    )
    copy.wait()


def per_device(points, vectors, leaf_interp, leaf_skeleton, group_transfer, group_skeleton):
    hbm = pl.BlockSpec(memory_space=pltpu.HBM)
    vmem = pl.BlockSpec(memory_space=pltpu.VMEM)
    dma = pltpu.SemaphoreType.DMA
    prod_t, gram = pl.pallas_call(
        main_kernel,
        out_shape=(jax.ShapeDtypeStruct((R, N), F32), jax.ShapeDtypeStruct((32, 128), F32)),
        in_specs=[hbm] * 6,
        out_specs=(vmem, vmem),
        scratch_shapes=[
            pltpu.VMEM((N, D), BF16),
            pltpu.VMEM((R, N), BF16),
            pltpu.VMEM((N, D), BF16),
            pltpu.VMEM((1, 128), jnp.int32),
            pltpu.VMEM((128, 512), BF16),
            pltpu.VMEM((1, 512), jnp.int32),
            pltpu.VMEM((SLOTS, BR, D), BF16),
            pltpu.VMEM((BR, D), BF16),
            pltpu.VMEM((2, BR, D), BF16),
            pltpu.VMEM((N, KR), BF16),
            pltpu.VMEM((N, R), F32),
            pltpu.VMEM((2, 8, 16, 128), F32),
            pltpu.VMEM((8, 16, 128), F32),
            pltpu.VMEM((2, 8, 32, 128), BF16),
            pltpu.VMEM((8, 32, 128), BF16),
            pltpu.VMEM((8, 16, 128), F32),
            pltpu.VMEM((8, 32, 128), BF16),
            pltpu.VMEM((16, 128), F32),
            pltpu.VMEM((32, 128), BF16),
            pltpu.VMEM((8, 48, 128), BF16),
            pltpu.VMEM((32, 128), F32),
            pltpu.VMEM((16, 128), F32),
            pltpu.VMEM((8, 16, 128), F32),
            pltpu.VMEM((16, 16, 128), F32),
            pltpu.VMEM((32, 128), F32),
            dma((6,)),
            dma((7,)),
            dma((7,)),
            dma((15,)),
            dma((15,)),
            dma((15,)),
            dma((15,)),
            dma((15,)),
            dma((2, 8)),
            dma((2, 8)),
            dma((8,)),
            dma((8,)),
            dma((14,)),
            dma((14,)),
            dma((14,)),
            dma((14,)),
            dma((8,)),
            dma((8,)),
            dma((15,)),
            dma((15,)),
        ],
        compiler_params=pltpu.CompilerParams(
            collective_id=0, has_side_effects=True, vmem_limit_bytes=40 * 2**20
        ),
        name="hss_main",
    )(
        *(
            pltpu.with_memory_space_constraint(a, pltpu.HBM)
            for a in (
                points,
                vectors.T,
                leaf_interp,
                leaf_skeleton.reshape(1, 128),
                group_transfer,
                group_skeleton.reshape(1, 512),
            )
        )
    )
    out_t, basis_t = pl.pallas_call(
        tail_kernel,
        out_shape=(jax.ShapeDtypeStruct((R, N), F32), jax.ShapeDtypeStruct((R, N), F32)),
        in_specs=[vmem, vmem],
        out_specs=(hbm, vmem),
        scratch_shapes=[pltpu.SemaphoreType.DMA],
        compiler_params=pltpu.CompilerParams(vmem_limit_bytes=16 * 2**20),
        name="hss_tail",
    )(prod_t, gram)
    return out_t.T, basis_t.T


def solution(mesh):
    spec = P(("group", "leaf"), None)
    return jax.shard_map(
        per_device,
        mesh=mesh,
        in_specs=(spec, spec, spec, P(("group", "leaf")), spec, P("group")),
        out_specs=(spec, spec),
        check_vma=False,
    )
```

time: 78.3 us -> 65.8 us (0.84)
  Pallas kernels: 73.1 us -> 65.1 us
  local copies, waits for them, and re-layouts: 4.38 us -> 0 us
    pallas_call x1, Pallas kernels: 7.44 us -> 2.84 us  [per_device(): pl.pallas_call(tail_kernel, out_shape=(jax.ShapeDtypeStruct((R, N), F32),...]
    unnamed x12 -> x0, local copies, waits for them, and re-layouts: 4.38 us -> none
    pallas_call x1, Pallas kernels: 65.7 us -> 62.3 us  [per_device(): pl.pallas_call(main_kernel, out_shape=(jax.ShapeDtypeStruct((R, N), F32),...]
where the time goes in v2:
time: 65.8 us; the launch traced here: 65.7 us
  Pallas kernels  65.1 us (99%)
    pallas_call x1, Pallas kernels, per_device(): pl.pallas_call(main_kernel, out_shape=(jax.ShapeDtypeStruct((R, N), F32),...  62.3 us
    pallas_call x1, Pallas kernels, per_device(): pl.pallas_call(tail_kernel, out_shape=(jax.ShapeDtypeStruct((R, N), F32),...  2.84 us

profile of v2, /device:TPU:1, one launch (start us, length us, event | category | flops | bytes accessed | tf_op | source)
XLA Modules:
  0.0 65.7 jit_solution(5436219786695577436)
XLA Ops:
  0.6 62.3 %hss_main.1 = (f32[64,1024]{1,0:T(8,128)S(1)}, f32[32,128]{1,0:T(8,128)S(1)}) custom-call(bf16[1024,128]{1,0:T(8,128)(2,1)} %pts_hbm.1, bf16[64,1024]{1,0:T(8,128)(2,1)} %bitcast.5, bf16[1024,128]{1,0:T(8,128)(2,1)} %interp_hbm.1, s32[1,128]{1,0:T(1,128)} %bitcast.7, bf16[128,512]{1,0:T(8,128)(2,1)} %trans_hbm.1, s32[1,512]{1,0:T(1,128)} %bitcast.6), custom_call_target="tpu_custom_call" | custom-call | tf_op jit(solution)/shard_map/hss_main/pallas_call | solution.py:416
  62.9 2.8 %hss_tail.1 = (f32[64,1024]{1,0:T(8,128)}, f32[64,1024]{1,0:T(8,128)}) custom-call(f32[64,1024]{1,0:T(8,128)S(1)} %get-tuple-element.6.prod_ref, f32[32,128]{1,0:T(8,128)S(1)} %get-tuple-element.7.gram_ref), custom_call_target="tpu_custom_call" | custom-call | tf_op jit(solution)/shard_map/hss_tail/pallas_call | solution.py:485

commit v3 on v2

--- a/solution.py
+++ b/solution.py
@@ -17,17 +17,17 @@
 KR = 144
 BR = KR + R
 NEAR = [
-    (1, 0), (7, 0), (0, 1), (2, 0), (6, 0), (1, 1), (7, 1), (3, 0),
-    (5, 0), (4, 0), (2, 1), (6, 1), (3, 1), (5, 1), (4, 1),
+    (1, 0), (7, 0), (0, 1), (2, 0), (6, 0), (1, 1), (7, 1), (2, 1),
+    (6, 1), (3, 0), (5, 0), (4, 0), (3, 1), (5, 1), (4, 1),
 ]
 FAR = [
-    ("y", 0, 1), ("y", 0, 3), ("x", 1, 0), ("x", 1, 1), ("x", 3, 0), ("x", 3, 1), ("y", 1, 1),
-    ("y", 1, 3), ("y", 3, 1), ("y", 3, 3), ("x", 2, 0), ("x", 2, 1), ("y", 2, 1), ("y", 2, 3),
+    ("y", 0, 1), ("y", 0, 3), ("x", 1, 0), ("x", 1, 1), ("x", 3, 0), ("x", 3, 1), ("x", 2, 0),
+    ("x", 2, 1), ("y", 1, 1), ("y", 1, 3), ("y", 3, 1), ("y", 3, 3), ("y", 2, 1), ("y", 2, 3),
 ]
 PLANE = [(dx, dyl, dyh) for dyl in range(2) for dyh in range(2) for dx in range(4) if (dx, dyl, dyh) != (0, 0, 0)]
 NEAR0 = 16
-FAR0 = 48
-SLOTS = 80
+FAR0 = 46
+SLOTS = 74
 
 
 def dot(a, b, ca=1, cb=0, precision=None):
@@ -55,8 +55,7 @@
     prod_ref, gram_ref,
     pts, vec, interp, lsk, trans, gsk, buf, own, far_own, q, acc,
     gw, gw_in, gp, gp_in, rsw, rsp, pair_in_w, pair_in_p, ag, g_loc, g_sib, g_z, g_p, g_half,
-    load_sem, sib_s, sib_r, near_s, near_r, nyh_s, nfw_s, nfw_r, rs_s, rs_r, zg_s, zg_r,
-    far_s, far_r, ffw_s, ffw_r, gz_s, gz_r, gp_s, gp_r,
+    load_sem, sib_s, sib_r, slot_s, near_r, nfw_r, far_r, ffw_r, rs_s, rs_r,
 ):
     grp = lax.axis_index("group")
     leaf = lax.axis_index("leaf")
@@ -93,7 +92,6 @@
     for p in peers:
         pl.semaphore_signal(barrier, inc=1, device_id=p, device_id_type=MESH)
     sib = dev(dc=1)
-    sent = []
 
     for c in loads:
         c.wait()
@@ -125,8 +123,6 @@
     q[:, 0:D] = pts[...] * jnp.asarray(1.0 / 32.0, BF16)
     q[:, D:KR] = jnp.transpose(norm_rows(pts_t, True))
     acc[...] = jnp.zeros_like(acc)
-    for s in (46, 47, 76, 77, 78, 79):
-        buf[s] = jnp.zeros((BR, D), BF16)
 
     pl.semaphore_wait(barrier, len(peers))
 
@@ -142,19 +138,24 @@
 
     def near_copy(k):
         dz, dyh = NEAR[k]
-        return remote(own, near_slot(k), near_s.at[k], near_r.at[k], dev(dz=dz and NZ - dz, dyh=dyh))
+        return remote(own, near_slot(k), slot_s.at[0], near_r.at[k], dev(dz=dz and NZ - dz, dyh=dyh))
 
     def near_yh(k):
         dz, _ = NEAR[k]
         j = NEAR.index((dz, 1))
-        return remote(near_slot(k), near_slot(j), nyh_s.at[k], near_r.at[j], dev(dyh=1))
+        return remote(near_slot(k), near_slot(j), slot_s.at[0], near_r.at[j], dev(dyh=1))
 
     def near_fwd(k):
-        return remote(near_slot(k), buf.at[NEAR0 + 2 * k + 1], nfw_s.at[k], nfw_r.at[k], sib)
+        return remote(near_slot(k), buf.at[NEAR0 + 2 * k + 1], slot_s.at[0], nfw_r.at[k // 4], sib)
 
     def start(make, *args):
         make(*args).start()
-        sent.append((make, args))
+
+    def arrived(ref, sem):
+        remote(ref, ref, sem, sem, sib).wait_recv()
+
+    def left(ref, sem):
+        remote(ref, ref, sem, sem, sib).wait_send()
 
     def near_arrived(k):
         near_copy(k).wait_recv()
@@ -163,10 +164,10 @@
             start(near_yh, k)
 
     def rs_w(d):
-        return remote(gw.at[core, lax.rem(z + d, NZ)], rsw.at[d], rs_s.at[0, d], rs_r.at[0, d], dev(dz=d))
+        return remote(gw.at[core, lax.rem(z + d, NZ)], rsw.at[d], rs_s.at[0], rs_r.at[0], dev(dz=d))
 
     def rs_p(d):
-        return remote(gp.at[core, lax.rem(z + d, NZ)], rsp.at[d], rs_s.at[1, d], rs_r.at[1, d], dev(dz=d))
+        return remote(gp.at[core, lax.rem(z + d, NZ)], rsp.at[d], rs_s.at[1], rs_r.at[1], dev(dz=d))
 
     def pair_w():
         return remote(rsw.at[0], pair_in_w, sib_s.at[5], sib_r.at[5], dev(dyh=1))
@@ -175,11 +176,7 @@
         return remote(rsp.at[0], pair_in_p, sib_s.at[6], sib_r.at[6], dev(dyh=1))
 
     def zg(d):
-        return remote(ag.at[z], ag.at[z], zg_s.at[d], zg_r.at[d], dev(dz=d))
-
-    def zg_wait(d):
-        theirs = ag.at[lax.rem(z + NZ - d, NZ)]
-        remote(theirs, theirs, zg_s.at[d], zg_r.at[d], dev(dz=d)).wait_recv()
+        return remote(ag.at[z], ag.at[z], rs_s.at[2], rs_r.at[2], dev(dz=d))
 
     def far_slot(k):
         return buf.at[FAR0 + 2 * k]
@@ -187,13 +184,13 @@
     def far_copy(k):
         axis, dx, n = FAR[k]
         if axis == "x":
-            return remote(far_own.at[n], far_slot(k), far_s.at[k], far_r.at[k], dev(dx=NX - dx))
+            return remote(far_own.at[n], far_slot(k), slot_s.at[0], far_r.at[k], dev(dx=NX - dx))
         quarter = 0 if n == 3 else 1
         src = far_own.at[quarter] if dx == 0 else far_slot(FAR.index(("x", dx, quarter)))
-        return remote(src, far_slot(k), far_s.at[k], far_r.at[k], ydev(4 - n))
+        return remote(src, far_slot(k), slot_s.at[0], far_r.at[k], ydev(4 - n))
 
     def far_fwd(k):
-        return remote(buf.at[FAR0 + 2 * k], buf.at[FAR0 + 2 * k + 1], ffw_s.at[k], ffw_r.at[k], sib)
+        return remote(buf.at[FAR0 + 2 * k], buf.at[FAR0 + 2 * k + 1], slot_s.at[0], ffw_r.at[(k + 3) // 4], sib)
 
     def phase_start():
         sib_w.wait_recv()
@@ -210,9 +207,8 @@
         sib_x.wait_recv()
 
     def phase_rs():
-        for d in range(1, 8):
-            rs_w(d).wait_recv()
-            rs_p(d).wait_recv()
+        arrived(rsw.at[pl.ds(1, 7)], rs_r.at[0])
+        arrived(rsp.at[pl.ds(1, 7)], rs_r.at[1])
         total = gw[core, z]
         rows = gp[core, z].astype(F32)
         for d in range(1, 8):
@@ -222,8 +218,9 @@
         rsp[0] = rows.astype(BF16)
         start(pair_w)
         start(pair_p)
-        for k in (7, 8, 9):
+        for k in (9, 10):
             start(near_copy, k)
+        near_arrive(0, 1, 2, 3, 4)
 
     def phase_pair():
         pair_w().wait_recv()
@@ -232,28 +229,29 @@
         ag[z, 16:48, :] = rsp[0] + pair_in_p[...]
         for d in range(1, 8):
             start(zg, d)
-
-    def near_phase(arrive, use):
-        for k in arrive:
+        start(near_copy, 11)
+        near_ready(0)
+
+    def near_arrive(*items):
+        for k in items:
             near_arrived(k)
-        for k in use:
-            near_fwd(k).wait_recv()
-
-    def phase_near0():
-        near_phase((0, 1, 2, 3, 4), (0, 1, 2, 3))
+
+    def near_ready(group):
+        arrived(buf.at[pl.ds(0, 3 if group == 3 else 4)], nfw_r.at[group])
 
     def phase_near1():
-        near_phase((7, 8, 9, 5, 6), (4, 5, 6, 7))
+        near_arrive(5, 6, 7, 8)
+        near_ready(1)
 
     def phase_near2():
-        near_phase((10, 11), (8, 9, 10, 11))
-
-    def phase_near3():
-        near_phase((12, 13, 14), (12, 13, 14))
+        near_arrive(9, 10)
+
+    def phase_near2b():
+        near_arrive(11)
+        near_ready(2)
 
     def phase_zg():
-        for d in range(1, 8):
-            zg_wait(d)
+        arrived(ag.at[pl.ds(0, 7)], rs_r.at[2])
         for n in range(2):
             points_t = jnp.concatenate([ag[t, 16 + n * 16 : 32 + n * 16, :] for t in range(NZ)], axis=0)
             far_own[n, 0:D, :] = points_t
@@ -267,50 +265,71 @@
             if axis == "x" or dx == 0:
                 start(far_copy, k)
 
-    def phase_far(arrive, use):
-        def far():
-            for k in arrive:
-                far_copy(k).wait_recv()
-                start(far_fwd, k)
-                axis, dx, n = FAR[k]
-                if axis == "x":
-                    start(far_copy, FAR.index(("y", dx, 3 if n == 0 else 1)))
-            for k in use:
-                far_fwd(k).wait_recv()
-
-        return far
+    def far_arrive(*items):
+        for k in items:
+            far_copy(k).wait_recv()
+            start(far_fwd, k)
+            axis, dx, n = FAR[k]
+            if axis == "x":
+                start(far_copy, FAR.index(("y", dx, 3 if n == 0 else 1)))
+
+    def far_ready(group):
+        arrived(buf.at[pl.ds(0, 4 if 0 < group < 4 else 1)], ffw_r.at[group])
+
+    def phase_far0():
+        far_arrive(0, 1, 2, 3, 4, 5)
+        near_arrive(12, 13, 14)
+        far_ready(1)
+
+    def phase_far1():
+        far_arrive(6, 7)
+        near_ready(3)
+        far_ready(0)
+
+    def phase_far2():
+        far_arrive(8, 9, 10, 11)
+        far_ready(2)
+
+    def phase_far3():
+        far_arrive(12, 13)
+        far_ready(3)
+
+    def phase_far4():
+        far_ready(4)
 
     with jax.named_scope("phase_start"):
         phase_start()
-    phases = [
-        (1, phase_sib),
-        (2, phase_rs),
-        (2, phase_near0),
-        (3, phase_pair),
-        (3, phase_near1),
-        (4, phase_zg),
-        (4, phase_near2),
-        (5, phase_near3),
-        (6, phase_far((0, 1, 2, 3, 4, 5), (0, 1, 2, 3))),
-        (7, phase_far((10, 11, 6, 7), (4, 5, 6, 7))),
-        (8, phase_far((8, 9), (8, 9, 10, 11))),
-        (9, phase_far((12, 13), (12, 13))),
+    steps = [
+        (0, []),
+        (1, [phase_sib]),
+        (2, [phase_rs, phase_pair]),
+        (3, [phase_near1]),
+        (4, [phase_near2, phase_zg, phase_near2b]),
+        (6, [phase_far0]),
+        (5, [phase_far1]),
+        (7, [phase_far2]),
+        (8, [phase_far3]),
     ]
 
     def chunk(i, carry):
-        for n, phase in phases:
-            with jax.named_scope(phase.__name__):
-                pl.when(i == n)(phase)
-        base = i * 8
-        keys = jnp.concatenate([buf[base + j, 0:KR, :] for j in range(8)], axis=1)
-        weights = jnp.concatenate([buf[base + j, KR:BR, :] for j in range(8)], axis=1)
+        for n, (_, phases) in enumerate(steps):
+            for phase in phases:
+                with jax.named_scope(phase.__name__):
+                    pl.when(i == n)(phase)
+        add_keys(jnp.where(i == 5, 6, jnp.where(i == 6, 5, i)) * 8, 8)
+        return carry
+
+    def add_keys(base, count):
+        keys = jnp.concatenate([buf[base + j, 0:KR, :] for j in range(count)], axis=1)
+        weights = jnp.concatenate([buf[base + j, KR:BR, :] for j in range(count)], axis=1)
         for t in range(4):
             rows = pl.ds(t * 256, 256)
             kernel_vals = jnp.exp(dot(q[rows, :], keys)).astype(BF16)
             acc[rows, :] += dot(kernel_vals, weights, 1, 1)
-        return carry
-
-    lax.fori_loop(0, 10, chunk, 0)
+
+    lax.fori_loop(0, 9, chunk, 0)
+    phase_far4()
+    add_keys(72, 2)
 
     prod_t = jnp.transpose(acc[...])
     prod_ref[...] = prod_t
@@ -320,11 +339,11 @@
         return remote(g_loc.at[pl.ds(other * 16, 16)], g_sib, sib_s.at[3], sib_r.at[3], sib)
 
     def gram_z(d):
-        return remote(g_z.at[z], g_z.at[z], gz_s.at[d], gz_r.at[d], dev(dz=d))
+        return remote(g_z.at[z], g_z.at[z], rs_s.at[3], rs_r.at[3], dev(dz=d))
 
     def gram_plane(k):
         dx, dyl, dyh = PLANE[k]
-        return remote(g_p.at[here], g_p.at[here], gp_s.at[k], gp_r.at[k], dev(dx=dx, dyl=dyl, dyh=dyh))
+        return remote(g_p.at[here], g_p.at[here], rs_s.at[4], rs_r.at[4], dev(dx=dx, dyl=dyl, dyh=dyh))
 
     def gram_back():
         mine = g_half.at[pl.ds(core * 16, 16)]
@@ -335,9 +354,13 @@
     g_z[z] = g_loc[pl.ds(core * 16, 16)] + g_sib[...]
     for d in range(1, 8):
         start(gram_z, d)
-    for d in range(1, 8):
-        fz = lax.rem(z + NZ - d, NZ)
-        remote(g_z.at[fz], g_z.at[fz], gz_s.at[d], gz_r.at[d], dev(dz=d)).wait_recv()
+    for c in (sib_w, sib_p, sib_x, pair_w(), pair_p()):
+        c.wait_send()
+    left(buf.at[pl.ds(0, 58)], slot_s.at[0])
+    left(rsw.at[pl.ds(1, 7)], rs_s.at[0])
+    left(rsp.at[pl.ds(1, 7)], rs_s.at[1])
+    left(ag.at[pl.ds(0, 7)], rs_s.at[2])
+    arrived(g_z.at[pl.ds(0, 7)], rs_r.at[3])
     total = g_z[0]
     for k in range(1, 8):
         total = total + g_z[k]
@@ -345,11 +368,7 @@
     g_p[here] = total
     for k in range(15):
         start(gram_plane, k)
-    for k, (dx, dyl, dyh) in enumerate(PLANE):
-        there = (lax.rem(yl + dyl, 2) * 2 + lax.rem(yh + dyh, 2)) * 4 + lax.rem(x + NX - dx, NX)
-        remote(
-            g_p.at[there], g_p.at[there], gp_s.at[k], gp_r.at[k], dev(dx=dx, dyl=dyl, dyh=dyh)
-        ).wait_recv()
+    arrived(g_p.at[pl.ds(0, 15)], rs_r.at[4])
     total = g_p[0]
     for k in range(1, 16):
         total = total + g_p[k]
@@ -358,10 +377,10 @@
     theirs = g_half.at[pl.ds(other * 16, 16)]
     remote(theirs, theirs, sib_s.at[4], sib_r.at[4], sib).wait_recv()
     gram_ref[...] = g_half[...]
-    for c in (sib_w, sib_p, sib_x):
-        c.wait_send()
-    for make, args in sent:
-        make(*args).wait_send()
+    gram_sib().wait_send()
+    gram_back().wait_send()
+    left(g_z.at[pl.ds(0, 7)], rs_s.at[3])
+    left(g_p.at[pl.ds(0, 15)], rs_s.at[4])
 
 
 def split(v):
@@ -447,23 +466,13 @@
             dma((6,)),
             dma((7,)),
             dma((7,)),
+            dma((1,)),
             dma((15,)),
-            dma((15,)),
-            dma((15,)),
-            dma((15,)),
-            dma((15,)),
-            dma((2, 8)),
-            dma((2, 8)),
-            dma((8,)),
-            dma((8,)),
+            dma((4,)),
             dma((14,)),
-            dma((14,)),
-            dma((14,)),
-            dma((14,)),
-            dma((8,)),
-            dma((8,)),
-            dma((15,)),
-            dma((15,)),
+            dma((5,)),
+            dma((5,)),
+            dma((5,)),
         ],
         compiler_params=pltpu.CompilerParams(
             collective_id=0, has_side_effects=True, vmem_limit_bytes=40 * 2**20

time: 65.8 us -> 60.1 us (0.913)
  Pallas kernels: 65.1 us -> 59.4 us
    pallas_call x1, Pallas kernels: 62.3 us -> 56.6 us  [per_device(): pl.pallas_call(main_kernel, out_shape=(jax.ShapeDtypeStruct((R, N), F32),...]
where the time goes in v3:
time: 60.1 us; the launch traced here: 60 us
  Pallas kernels  59.4 us (99%)
  between operations  0.64 us (1%)
    pallas_call x1, Pallas kernels, per_device(): pl.pallas_call(main_kernel, out_shape=(jax.ShapeDtypeStruct((R, N), F32),...  56.6 us
    pallas_call x1, Pallas kernels, per_device(): pl.pallas_call(tail_kernel, out_shape=(jax.ShapeDtypeStruct((R, N), F32),...  2.84 us

profile of v3, /device:TPU:1, one launch (start us, length us, event | category | flops | bytes accessed | tf_op | source)
XLA Modules:
  0.0 60.0 jit_solution(9754214108295304013)
XLA Ops:
  0.6 56.6 %hss_main.1 = (f32[64,1024]{1,0:T(8,128)S(1)}, f32[32,128]{1,0:T(8,128)S(1)}) custom-call(bf16[1024,128]{1,0:T(8,128)(2,1)} %pts_hbm.1, bf16[64,1024]{1,0:T(8,128)(2,1)} %bitcast.5, bf16[1024,128]{1,0:T(8,128)(2,1)} %interp_hbm.1, s32[1,128]{1,0:T(1,128)} %bitcast.7, bf16[128,512]{1,0:T(8,128)(2,1)} %trans_hbm.1, s32[1,512]{1,0:T(1,128)} %bitcast.6), custom_call_target="tpu_custom_call" | custom-call | tf_op jit(solution)/shard_map/hss_main/pallas_call | solution.py:435
  57.2 2.8 %hss_tail.1 = (f32[64,1024]{1,0:T(8,128)}, f32[64,1024]{1,0:T(8,128)}) custom-call(f32[64,1024]{1,0:T(8,128)S(1)} %get-tuple-element.6.prod_ref, f32[32,128]{1,0:T(8,128)S(1)} %get-tuple-element.7.gram_ref), custom_call_target="tpu_custom_call" | custom-call | tf_op jit(solution)/shard_map/hss_tail/pallas_call | solution.py:494

commit v4 on v3

--- a/solution.py
+++ b/solution.py
@@ -17,7 +17,7 @@
 KR = 144
 BR = KR + R
 NEAR = [
-    (1, 0), (7, 0), (0, 1), (2, 0), (6, 0), (1, 1), (7, 1), (2, 1),
+    (1, 0), (7, 0), (0, 1), (1, 1), (7, 1), (2, 0), (6, 0), (2, 1),
     (6, 1), (3, 0), (5, 0), (4, 0), (3, 1), (5, 1), (4, 1),
 ]
 FAR = [
@@ -140,13 +140,22 @@
         dz, dyh = NEAR[k]
         return remote(own, near_slot(k), slot_s.at[0], near_r.at[k], dev(dz=dz and NZ - dz, dyh=dyh))
 
-    def near_yh(k):
-        dz, _ = NEAR[k]
+    def near_along(k):
+        dz, dyh = NEAR[k]
+        j = NEAR.index((dz + 1 if dz < 4 else dz - 1, dyh))
+        return remote(near_slot(k), near_slot(j), slot_s.at[0], near_r.at[j], dev(dz=7 if dz < 4 else 1))
+
+    def near_beside(dz):
         j = NEAR.index((dz, 1))
-        return remote(near_slot(k), near_slot(j), slot_s.at[0], near_r.at[j], dev(dyh=1))
+        return remote(near_slot(2), near_slot(j), slot_s.at[0], near_r.at[j], dev(dz=NZ - dz))
+
+    def near_across(k):
+        j = NEAR.index((4, NEAR[k][1]))
+        src = buf.at[NEAR0 + 2 * k + 2 * core]
+        return remote(src, near_slot(j), slot_s.at[0], near_r.at[j], dev(dz=6 - 4 * core))
 
     def near_fwd(k):
-        return remote(near_slot(k), buf.at[NEAR0 + 2 * k + 1], slot_s.at[0], nfw_r.at[k // 4], sib)
+        return remote(near_slot(k), buf.at[NEAR0 + 2 * k + 1], slot_s.at[0], nfw_r.at[(k + 1) // 4], sib)
 
     def start(make, *args):
         make(*args).start()
@@ -160,8 +169,13 @@
     def near_arrived(k):
         near_copy(k).wait_recv()
         start(near_fwd, k)
-        if NEAR[k][1] == 0:
-            start(near_yh, k)
+        if NEAR[k][0] in (1, 2, 6, 7):
+            start(near_along, k)
+        if NEAR[k][0] == 6:
+            start(near_across, k - 1)
+        if k == 2:
+            start(near_beside, 1)
+            start(near_beside, 7)
 
     def rs_w(d):
         return remote(gw.at[core, lax.rem(z + d, NZ)], rsw.at[d], rs_s.at[0], rs_r.at[0], dev(dz=d))
@@ -190,7 +204,7 @@
         return remote(src, far_slot(k), slot_s.at[0], far_r.at[k], ydev(4 - n))
 
     def far_fwd(k):
-        return remote(buf.at[FAR0 + 2 * k], buf.at[FAR0 + 2 * k + 1], slot_s.at[0], ffw_r.at[(k + 3) // 4], sib)
+        return remote(buf.at[FAR0 + 2 * k], buf.at[FAR0 + 2 * k + 1], slot_s.at[0], ffw_r.at[k // 4], sib)
 
     def phase_start():
         sib_w.wait_recv()
@@ -200,7 +214,7 @@
         for d in range(1, 8):
             start(rs_w, d)
             start(rs_p, d)
-        for k in (0, 1, 2, 3, 4):
+        for k in (0, 1, 2):
             start(near_copy, k)
 
     def phase_sib():
@@ -218,9 +232,11 @@
         rsp[0] = rows.astype(BF16)
         start(pair_w)
         start(pair_p)
-        for k in (9, 10):
-            start(near_copy, k)
-        near_arrive(0, 1, 2, 3, 4)
+        near_arrive(0, 1, 2)
+        near_ready(0)
+
+    def step_near0():
+        add_keys(16, 6)
 
     def phase_pair():
         pair_w().wait_recv()
@@ -229,26 +245,23 @@
         ag[z, 16:48, :] = rsp[0] + pair_in_p[...]
         for d in range(1, 8):
             start(zg, d)
-        start(near_copy, 11)
-        near_ready(0)
+        near_arrive(3, 4, 5, 6)
+        near_ready(1)
 
     def near_arrive(*items):
         for k in items:
             near_arrived(k)
 
     def near_ready(group):
-        arrived(buf.at[pl.ds(0, 3 if group == 3 else 4)], nfw_r.at[group])
-
-    def phase_near1():
-        near_arrive(5, 6, 7, 8)
-        near_ready(1)
+        arrived(buf.at[pl.ds(0, 4 if group else 3)], nfw_r.at[group])
 
     def phase_near2():
-        near_arrive(9, 10)
-
-    def phase_near2b():
-        near_arrive(11)
+        near_arrive(7, 8, 9, 10)
         near_ready(2)
+
+    def phase_near3():
+        near_arrive(11, 12, 13, 14)
+        near_ready(3)
 
     def phase_zg():
         arrived(ag.at[pl.ds(0, 7)], rs_r.at[2])
@@ -269,46 +282,47 @@
         for k in items:
             far_copy(k).wait_recv()
             start(far_fwd, k)
+        for k in items:
             axis, dx, n = FAR[k]
             if axis == "x":
                 start(far_copy, FAR.index(("y", dx, 3 if n == 0 else 1)))
 
     def far_ready(group):
-        arrived(buf.at[pl.ds(0, 4 if 0 < group < 4 else 1)], ffw_r.at[group])
+        arrived(buf.at[pl.ds(0, 2 if group == 3 else 4)], ffw_r.at[group])
 
     def phase_far0():
         far_arrive(0, 1, 2, 3, 4, 5)
-        near_arrive(12, 13, 14)
-        far_ready(1)
 
     def phase_far1():
         far_arrive(6, 7)
-        near_ready(3)
+
+    def phase_far1b():
         far_ready(0)
 
     def phase_far2():
         far_arrive(8, 9, 10, 11)
+
+    def phase_far2b():
+        far_ready(1)
+
+    def phase_far2c():
+        far_arrive(12, 13)
         far_ready(2)
 
     def phase_far3():
-        far_arrive(12, 13)
         far_ready(3)
-
-    def phase_far4():
-        far_ready(4)
 
     with jax.named_scope("phase_start"):
         phase_start()
     steps = [
         (0, []),
         (1, [phase_sib]),
-        (2, [phase_rs, phase_pair]),
-        (3, [phase_near1]),
-        (4, [phase_near2, phase_zg, phase_near2b]),
-        (6, [phase_far0]),
-        (5, [phase_far1]),
-        (7, [phase_far2]),
-        (8, [phase_far3]),
+        (2, [phase_rs, step_near0, phase_pair]),
+        (3, [phase_zg, phase_near2]),
+        (4, [phase_far0, phase_near3]),
+        (5, [phase_far1, phase_far1b]),
+        (6, [phase_far2, phase_far2b]),
+        (7, [phase_far2c]),
     ]
 
     def chunk(i, carry):
@@ -316,7 +330,7 @@
             for phase in phases:
                 with jax.named_scope(phase.__name__):
                     pl.when(i == n)(phase)
-        add_keys(jnp.where(i == 5, 6, jnp.where(i == 6, 5, i)) * 8, 8)
+        add_keys(jnp.where(i < 2, i * 8, i * 8 + 6), 8)
         return carry
 
     def add_keys(base, count):
@@ -327,9 +341,10 @@
             kernel_vals = jnp.exp(dot(q[rows, :], keys)).astype(BF16)
             acc[rows, :] += dot(kernel_vals, weights, 1, 1)
 
-    lax.fori_loop(0, 9, chunk, 0)
-    phase_far4()
-    add_keys(72, 2)
+    lax.fori_loop(0, 8, chunk, 0)
+    with jax.named_scope("phase_far3"):
+        phase_far3()
+    add_keys(70, 4)
 
     prod_t = jnp.transpose(acc[...])
     prod_ref[...] = prod_t
@@ -470,7 +485,7 @@
             dma((15,)),
             dma((4,)),
             dma((14,)),
-            dma((5,)),
+            dma((4,)),
             dma((5,)),
             dma((5,)),
         ],

time: 60.1 us -> 57.5 us (0.957)
  Pallas kernels: 59.4 us -> 56.8 us
    pallas_call x1, Pallas kernels: 56.6 us -> 53.9 us  [per_device(): pl.pallas_call(main_kernel, out_shape=(jax.ShapeDtypeStruct((R, N), F32),...]
where the time goes in v4:
time: 57.5 us; the launch traced here: 57.4 us
  Pallas kernels  56.8 us (99%)
  between operations  0.64 us (1%)
    pallas_call x1, Pallas kernels, per_device(): pl.pallas_call(main_kernel, out_shape=(jax.ShapeDtypeStruct((R, N), F32),...  53.9 us
    pallas_call x1, Pallas kernels, per_device(): pl.pallas_call(tail_kernel, out_shape=(jax.ShapeDtypeStruct((R, N), F32),...  2.84 us

profile of v4, /device:TPU:1, one launch (start us, length us, event | category | flops | bytes accessed | tf_op | source)
XLA Modules:
  0.0 57.4 jit_solution(15127263988923654277)
XLA Ops:
  0.6 53.9 %hss_main.1 = (f32[64,1024]{1,0:T(8,128)S(1)}, f32[32,128]{1,0:T(8,128)S(1)}) custom-call(bf16[1024,128]{1,0:T(8,128)(2,1)} %pts_hbm.1, bf16[64,1024]{1,0:T(8,128)(2,1)} %bitcast.5, bf16[1024,128]{1,0:T(8,128)(2,1)} %interp_hbm.1, s32[1,128]{1,0:T(1,128)} %bitcast.7, bf16[128,512]{1,0:T(8,128)(2,1)} %trans_hbm.1, s32[1,512]{1,0:T(1,128)} %bitcast.6), custom_call_target="tpu_custom_call" | custom-call | tf_op jit(solution)/shard_map/hss_main/pallas_call | solution.py:450
  54.6 2.8 %hss_tail.1 = (f32[64,1024]{1,0:T(8,128)}, f32[64,1024]{1,0:T(8,128)}) custom-call(f32[64,1024]{1,0:T(8,128)S(1)} %get-tuple-element.6.prod_ref, f32[32,128]{1,0:T(8,128)S(1)} %get-tuple-element.7.gram_ref), custom_call_target="tpu_custom_call" | custom-call | tf_op jit(solution)/shard_map/hss_tail/pallas_call | solution.py:509

commit v5 on v4

--- a/solution.py
+++ b/solution.py
@@ -24,7 +24,13 @@
     ("y", 0, 1), ("y", 0, 3), ("x", 1, 0), ("x", 1, 1), ("x", 3, 0), ("x", 3, 1), ("x", 2, 0),
     ("x", 2, 1), ("y", 1, 1), ("y", 1, 3), ("y", 3, 1), ("y", 3, 3), ("y", 2, 1), ("y", 2, 3),
 ]
-PLANE = [(dx, dyl, dyh) for dyl in range(2) for dyh in range(2) for dx in range(4) if (dx, dyl, dyh) != (0, 0, 0)]
+PLANE = [
+    (dx, dyl, dyh)
+    for dx in (2, 1, 3, 0)
+    for dyl, dyh in ((0, 1), (1, 0), (1, 1), (0, 0))
+    if (dx, dyl, dyh) != (0, 0, 0)
+]
+FARTHEST = (4, 3, 5, 2, 6, 1, 7)
 NEAR0 = 16
 FAR0 = 46
 SLOTS = 74
@@ -130,7 +136,7 @@
     sib_w = remote(gw.at[other], gw_in, sib_s.at[0], sib_r.at[0], sib)
     sib_p = remote(gp.at[other], gp_in, sib_s.at[1], sib_r.at[1], sib)
     sib_x = remote(buf.at[pl.ds(0, 8)], buf.at[pl.ds(8, 8)], sib_s.at[2], sib_r.at[2], sib)
-    for c in (sib_w, sib_p, sib_x):
+    for c in (sib_w, sib_p):
         c.start()
 
     def near_slot(k):
@@ -211,9 +217,10 @@
         sib_p.wait_recv()
         gw[core] = gw[core] + gw_in[...]
         gp[core] = gp[core] + gp_in[...]
-        for d in range(1, 8):
+        for d in FARTHEST:
             start(rs_w, d)
             start(rs_p, d)
+        sib_x.start()
         for k in (0, 1, 2):
             start(near_copy, k)
 
@@ -243,7 +250,7 @@
         pair_p().wait_recv()
         ag[z, 0:16, :] = (rsw[0] + pair_in_w[...]).astype(BF16)
         ag[z, 16:48, :] = rsp[0] + pair_in_p[...]
-        for d in range(1, 8):
+        for d in FARTHEST:
             start(zg, d)
         near_arrive(3, 4, 5, 6)
         near_ready(1)
@@ -274,9 +281,8 @@
             )
             w_pairs = jnp.transpose(pairs)
             far_own[n, KR:BR, :] = jnp.concatenate([w_pairs[0:R], w_pairs[R : 2 * R]], axis=1).astype(BF16)
-        for k, (axis, dx, _) in enumerate(FAR):
-            if axis == "x" or dx == 0:
-                start(far_copy, k)
+        for k in (2, 4, 3, 5, 6, 7, 0, 1):
+            start(far_copy, k)
 
     def far_arrive(*items):
         for k in items:
@@ -367,7 +373,7 @@
     start(gram_sib)
     gram_sib().wait_recv()
     g_z[z] = g_loc[pl.ds(core * 16, 16)] + g_sib[...]
-    for d in range(1, 8):
+    for d in FARTHEST:
         start(gram_z, d)
     for c in (sib_w, sib_p, sib_x, pair_w(), pair_p()):
         c.wait_send()

time: 57.5 us -> 56.2 us (0.977)
  Pallas kernels: 56.8 us -> 55.4 us
    pallas_call x1, Pallas kernels: 53.9 us -> 52.6 us  [per_device(): pl.pallas_call(main_kernel, out_shape=(jax.ShapeDtypeStruct((R, N), F32),...]
where the time goes in v5:
time: 56.2 us; the launch traced here: 56.1 us
  Pallas kernels  55.4 us (99%)
  between operations  0.64 us (1%)
    pallas_call x1, Pallas kernels, per_device(): pl.pallas_call(main_kernel, out_shape=(jax.ShapeDtypeStruct((R, N), F32),...  52.6 us
    pallas_call x1, Pallas kernels, per_device(): pl.pallas_call(tail_kernel, out_shape=(jax.ShapeDtypeStruct((R, N), F32),...  2.84 us

profile of v5, /device:TPU:1, one launch (start us, length us, event | category | flops | bytes accessed | tf_op | source)
XLA Modules:
  0.0 56.1 jit_solution(5252167675041054411)
XLA Ops:
  0.6 52.6 %hss_main.1 = (f32[64,1024]{1,0:T(8,128)S(1)}, f32[32,128]{1,0:T(8,128)S(1)}) custom-call(bf16[1024,128]{1,0:T(8,128)(2,1)} %pts_hbm.1, bf16[64,1024]{1,0:T(8,128)(2,1)} %bitcast.5, bf16[1024,128]{1,0:T(8,128)(2,1)} %interp_hbm.1, s32[1,128]{1,0:T(1,128)} %bitcast.7, bf16[128,512]{1,0:T(8,128)(2,1)} %trans_hbm.1, s32[1,512]{1,0:T(1,128)} %bitcast.6), custom_call_target="tpu_custom_call" | custom-call | tf_op jit(solution)/shard_map/hss_main/pallas_call | solution.py:456
  53.2 2.8 %hss_tail.1 = (f32[64,1024]{1,0:T(8,128)}, f32[64,1024]{1,0:T(8,128)}) custom-call(f32[64,1024]{1,0:T(8,128)S(1)} %get-tuple-element.6.prod_ref, f32[32,128]{1,0:T(8,128)S(1)} %get-tuple-element.7.gram_ref), custom_call_target="tpu_custom_call" | custom-call | tf_op jit(solution)/shard_map/hss_tail/pallas_call | solution.py:515
